TPU v7x, 128 devices: a whole 4x4x4 slice. The times are simulated.
128 devices in a mesh: seq: 16 (over y, z), dec: 8 (over x, core).
Axes of the slice: x: 4, y: 4, z: 4, core: 2. Of those that a mesh axis runs over, the one named last changes fastest.
Arguments:
- query_nope: bfloat16 [8192, 16384], P('seq', 'dec'), may hold values from -6 to 6
- query_rope: bfloat16 [8192, 8192], P('seq', 'dec'), may hold values from -8 to 8
- latent_cache: bfloat16 [8192, 576], P(('seq', 'dec')), may hold values from -8 to 8
- key_up: bfloat16 [128, 128, 512], P('dec'), may hold values from -0.5 to 0.5
- value_up: bfloat16 [128, 512, 128], P('dec'), may hold values from -1 to 1
- vertical_lists: int32 [8, 256, 4], replicated, may hold values from 0 to 255, as said below
- page_owner: int32 [256, 1], replicated, may hold values from 0 to 7; in each aligned block of 16 rows (0 to 15, 16 to 31, ...) at most 3 rows name the same one
- step_nope: bfloat16 [64, 2, 16384], P('seq', None, 'dec'), may hold values from -6 to 6
- step_rope: bfloat16 [64, 2, 8192], P('seq', None, 'dec'), may hold values from -8 to 8
- step_latent: bfloat16 [64, 2, 576], P('seq'), may hold values from -6 to 6
- prefix_lengths: int32 [64], P('seq'), may hold values from 64 to 8192, as said below
Outputs:
- prefill_out: bfloat16 [8192, 16384], P('seq', 'dec')
- paged_cache: bfloat16 [8, 48, 32, 576], P('dec')
- decode_out: bfloat16 [64, 2, 16384], P('seq', None, 'dec')
Inputs may be any that keep to these rules, and one draw needn't show every extreme that they name: `vertical_lists`: block numbers. The 64 entries of one head group for the query blocks of one seq index all differ; at most 1 of them name blocks k with the same k // 2, and 1 is reached. An entry may exceed its query block minus 3 only when no block at or before that limit can still be listed under the bound above; such entries are listed but not attended. `page_owner`: within the pages of one seq index (aligned blocks of 16 pages) no value appears more than 3 times, and 3 is reached. `prefix_lengths`: 8192 is reached.
All inputs are finite; a program needn't handle non-finite values.
Results may differ from a plain program's by a relative error of at most 0.0069.
Values may be sent and summed in bfloat16 or wider, within the bound.
A program may use at most 128 MiB of HBM per device.

v0:
```python
import jax
import jax.numpy as jnp
from jax import lax
from jax.experimental import pallas as pl
from jax.experimental.pallas import tpu as pltpu
from jax.sharding import PartitionSpec as P

MESH = pl.DeviceIdType.MESH
ORDERS = (("x", "y", "z"), ("y", "z", "x"), ("z", "x", "y"))
ALL = slice(None)
COPIES = 200


class Gather:
    def __init__(self, cache, send, recv):
        seq, dec = lax.axis_index("seq"), lax.axis_index("dec")
        self.at = {"x": dec // 2, "y": seq // 4, "z": seq % 4}
        self.core = dec % 2
        self.cache, self.send, self.recv = cache, send, recv
        self.own = None
        self.sent, self.number, self.shares = [], {}, []

    def device(self, axis=None, by=0, mate=False):
        at = dict(self.at)
        if axis is not None:
            at[axis] = (at[axis] + by + 4) % 4
        core = 1 - self.core if mate else self.core
        return (at["y"] * 4 + at["z"], at["x"] * 2 + core)

    def slot(self, mate=False):
        core = 1 - self.core if mate else self.core
        return self.cache.at[self.at["y"], self.at["z"], self.at["x"], core]

    def chunk(self, g, rel, mate=False):
        where = []
        for axis in ("y", "z", "x"):
            r = rel[ORDERS[g].index(axis)]
            where.append(r if isinstance(r, slice) else (self.at[axis] + r + 4) % 4)
        core = 1 - self.core if mate else self.core
        return self.cache.at[where[0], where[1], where[2], core, pl.ds(6 * g, 6)]

    def copy(self, key, src, dst, target):
        k = self.number.setdefault(key, len(self.number))
        return pltpu.make_async_remote_copy(
            src_ref=src, dst_ref=dst, send_sem=self.send.at[k], recv_sem=self.recv.at[k],
            device_id=target, device_id_type=MESH)

    def hop(self, g, phase, rel, by):
        dst = self.chunk(g, rel)
        src = self.own.at[pl.ds(6 * g, 6)] if rel == (0, 0, 0) else dst
        key = (g, phase) + tuple(map(str, rel)) + (by,)
        copy = self.copy(key, src, dst, self.device(ORDERS[g][phase], by))
        copy.start()
        self.sent.append(copy)

    def land(self, g, phase, rel, by):
        got = list(rel)
        got[phase] = {0: -by, -by: 2}[rel[phase]]
        if got[phase] == -2:
            got[phase] = 2
        dst = self.chunk(g, got)
        key = (g, phase) + tuple(map(str, rel)) + (by,)
        self.copy(key, dst, dst, self.device(mate=True)).wait_recv()
        return tuple(got)

    def give(self, g, rel):
        src = self.chunk(g, rel)
        key = ("core", g) + tuple(map(str, rel))
        copy = self.copy(key, src, src, self.device(mate=True))
        copy.start()
        self.sent.append(copy)
        self.shares.append((key, self.chunk(g, rel, mate=True)))

    def give_own(self):
        copy = self.copy(("core",), self.own, self.slot(), self.device(mate=True))
        copy.start()
        self.sent.append(copy)
        self.shares.append((("core",), self.slot(mate=True)))

    def take(self):
        for key, ref in self.shares:
            self.copy(key, ref, ref, self.device(mate=True)).wait_recv()

    def barrier_start(self):
        sem = pltpu.get_barrier_semaphore()
        for axis in ("x", "y", "z"):
            for by in (-1, 1, 2):
                pl.semaphore_signal(sem, inc=1, device_id=self.device(axis, by), device_id_type=MESH)
        pl.semaphore_signal(sem, inc=1, device_id=self.device(mate=True), device_id_type=MESH)

    def barrier_wait(self):
        pl.semaphore_wait(pltpu.get_barrier_semaphore(), 10)

    def steps(self):
        three = range(3)
        near = (1, -1)
        for phase in (0, 1):
            for g in three:
                for by in near + (2,):
                    self.hop(g, phase, (0, 0, 0), by)
        for g in three:
            for by in near:
                self.hop(g, 2, (0, 0, 0), by)
        self.give_own()
        yield "own"
        for by in near + (2,):
            for g in three:
                got = self.land(g, 0, (0, 0, 0), by)
                for way in near + (2,):
                    self.hop(g, 1, got, way)
            yield "first"
        for by in near + (2,):
            for g in three:
                got = (-by if by != 2 else 2, 0, 0)
                for way in near:
                    self.hop(g, 2, got, way)
                self.give(g, got)
        yield "first"
        for by in near + (2,):
            for g in three:
                for r1 in (0, 1, -1, 2):
                    got = self.land(g, 1, (r1, 0, 0), by)
                got = (ALL,) + got[1:]
                for way in near:
                    self.hop(g, 2, got, way)
                self.give(g, got)
            yield "second"
        for g in three:
            for r1, on in ((0, 1), (1, -1), (-1, 1), (2, -1)):
                for by in near:
                    got = self.land(g, 2, (r1, 0, 0), by)
                    if by == on:
                        self.hop(g, 2, got, by)
            for r3 in near:
                self.give(g, (ALL, 0, r3))
            yield "third"
        for r2 in near + (2,):
            for g in three:
                for by in near:
                    got = self.land(g, 2, (ALL, r2, 0), by)
                    if r2 == 2:
                        self.hop(g, 2, (slice(0, 2) if by == 1 else slice(2, 4),) + got[1:], by)
                    elif r2 == by:
                        self.hop(g, 2, got, by)
                    self.give(g, got)
                yield "third"
        for g in three:
            for r1, on in ((0, 1), (1, -1), (-1, 1), (2, -1)):
                self.land(g, 2, (r1, 0, -on), on)
            self.give(g, (ALL, 0, 2))
        yield "far"
        for r2 in near:
            for g in three:
                self.give(g, self.land(g, 2, (ALL, r2, -r2), r2))
            yield "far"
        for g in three:
            self.land(g, 2, (slice(0, 2), 2, -1), 1)
            self.land(g, 2, (slice(2, 4), 2, 1), -1)
            self.give(g, (ALL, 2, 2))
        yield "far"
        self.take()
        for copy in self.sent:
            copy.wait_send()
        yield "all"


BLK = 32
VB = 4
SLASH = 2
TILES = 9
HALF = 8
SCALE = 192.0 ** -0.5
EXP2 = SCALE * 1.4426950408889634
NEG = float("-inf")


def dot(a, b):
    return jnp.dot(a, b, preferred_element_type=jnp.float32)


def dot_t(a, b):
    return lax.dot_general(a, b, (((1,), (1,)), ((), ())), preferred_element_type=jnp.float32)


def even_first(h):
    return (h % 2) * HALF + h // 2


def pack(rows, tiles):
    for b in range(2):
        for r in range(2):
            start = 32 * b + 16 * r
            for c in range(4):
                tiles[9 * b + 4 * r + c] = rows[start : start + 16, 128 * c : 128 * c + 128]
        tiles[9 * b + 8] = jnp.concatenate(
            [rows[32 * b : 32 * b + 16, 512:576], rows[32 * b + 16 : 32 * b + 32, 512:576]], axis=1
        )


def rope_pair(tile):
    swapped = jnp.concatenate([tile[..., 64:], tile[..., :64]], axis=-1)
    low = lax.broadcasted_iota(jnp.int32, tile.shape, tile.ndim - 1) < 64
    zero = jnp.zeros_like(tile)
    first = (jnp.where(low, tile, zero), jnp.where(low, swapped, zero))
    second = (jnp.where(low, zero, swapped), jnp.where(low, zero, tile))
    return first, second


def gather_kernel(
    prefix, latent, step_nope, step_rope, step_latent, query_nope, key_up,
    cache, absorbed, decoded,
    tiles, qn, ku, hold, chunk, keys, rope, dq, dr, acc, top, total,
    send, recv, local, held, loaded,
):
    t = Gather(cache, send, recv)
    t.barrier_start()
    in_q = pltpu.make_async_copy(query_nope, qn, local.at[0])
    in_k = pltpu.make_async_copy(key_up, ku, local.at[1])
    in_q.start()
    in_k.start()
    pack(latent, tiles)
    t.barrier_wait()
    t.own = tiles
    own_copy = pltpu.make_async_copy(tiles, t.slot(), local.at[2])
    own_copy.start()

    copies = [None, None]

    def absorb(h):
        if h == 0:
            in_q.wait()
            in_k.wait()
        slot = h % 2
        if copies[slot] is not None:
            copies[slot].wait()
        got = dot(qn[:, 128 * h : 128 * h + 128], ku[h]).astype(jnp.bfloat16)
        hold[slot] = got.reshape(16, BLK, 512)
        copies[slot] = pltpu.make_async_copy(hold.at[slot], absorbed.at[:, even_first(h)], held.at[slot])
        copies[slot].start()

    def decode_start():
        for p in range(HALF):
            for odd in range(2):
                h = 2 * p + odd
                dq[odd, p] = dot(step_nope[:, 128 * h : 128 * h + 128], ku[h])
            dr[p] = step_rope[:, 128 * p : 128 * p + 128].astype(jnp.float32)
        q = dq[...].reshape(128, 512).astype(jnp.bfloat16)
        r = dr[...].reshape(64, 128).astype(jnp.bfloat16)
        fresh = step_latent[...]
        fr = fresh[:, 512:576]
        zero = jnp.zeros((8, 64), jnp.bfloat16)
        even = dot_t(r, jnp.concatenate([fr, zero], axis=1))
        odd = dot_t(r, jnp.concatenate([zero, fr], axis=1))
        s = dot_t(q, fresh[:, :512]) + jnp.concatenate([even, odd], axis=0)
        row = lax.broadcasted_iota(jnp.int32, (128, 8), 0) % 8
        key = lax.broadcasted_iota(jnp.int32, (128, 8), 1)
        s = jnp.where((row // 2 == key // 2) & (key <= row), s, NEG)
        m = jnp.max(s, axis=1, keepdims=True)
        e = jnp.exp2((s - m) * EXP2)
        top[...] = jnp.broadcast_to(m, (128, 128))
        total[...] = jnp.broadcast_to(jnp.sum(e, axis=1, keepdims=True), (128, 128))
        acc[...] = dot(e.astype(jnp.bfloat16), fresh[:, :512])

    def load(n):
        return pltpu.make_async_copy(cache.at[n // 4, n % 4], chunk.at[n % 2], loaded.at[n % 2])

    def decode(n):
        for x in range(4):
            for c in range(2):
                for b in range(2):
                    blk = (x * 2 + c) * 2 + b
                    for r in range(2):
                        at = 32 * blk + 16 * r
                        for w in range(4):
                            keys[at : at + 16, 128 * w : 128 * w + 128] = chunk[n % 2, x, c, 9 * b + 4 * r + w]
                    first, second = rope_pair(chunk[n % 2, x, c, 9 * b + 8])
                    for r in range(2):
                        at = 32 * blk + 16 * r
                        rope[0, at : at + 16] = first[r]
                        rope[1, at : at + 16] = second[r]
        q = dq[...].reshape(128, 512).astype(jnp.bfloat16)
        r = dr[...].reshape(64, 128).astype(jnp.bfloat16)
        s = dot_t(q, keys[...]) + jnp.concatenate([dot_t(r, rope[0]), dot_t(r, rope[1])], axis=0)
        row = lax.broadcasted_iota(jnp.int32, (128, 512), 0) % 8 // 2
        limit = jnp.where(row == 0, prefix[0], jnp.where(row == 1, prefix[1], jnp.where(row == 2, prefix[2], prefix[3])))
        place = lax.broadcasted_iota(jnp.int32, (128, 512), 1) + 512 * n
        s = jnp.where(place < limit, s, NEG)
        before = top[:, :1]
        m = jnp.maximum(before, jnp.max(s, axis=1, keepdims=True))
        keep = jnp.exp2((before - m) * EXP2)
        e = jnp.exp2((s - m) * EXP2)
        top[...] = jnp.broadcast_to(m, (128, 128))
        total[...] = total[...] * keep + jnp.sum(e, axis=1, keepdims=True)
        acc[...] = acc[...] * keep + dot(e.astype(jnp.bfloat16), keys[...])

    step = 0
    for name in t.steps():
        if step < 8:
            absorb(2 * step)
            absorb(2 * step + 1)
        elif step == 8:
            decode_start()
        step += 1
    own_copy.wait()
    for c in copies:
        c.wait()
    load(0).start()
    for n in range(16):
        if n < 15:
            load(n + 1).start()
        load(n).wait()
        decode(n)
    decoded[...] = (acc[...] / total[:, :1]).reshape(2, HALF, 8, 512)


def attend_kernel(
    listed, slots, cache, absorbed, query_rope, value_up, decoded,
    prefill_out, paged, decode_out,
    near, far, qa, qr, vu, pages, keys, rope, ctx, out, paged_hold,
    s_near, s_far, s_qa, s_in, s_page, s_out, s_paged,
):
    seq = lax.axis_index("seq")
    own = [
        pltpu.make_async_copy(cache.at[pl.ds(seq * 16, 16)], near.at[pl.ds(2, 16)], s_near.at[0]),
        pltpu.make_async_copy(cache.at[pl.ds(jnp.maximum(seq * 16 - 2, 0), 2)], near.at[pl.ds(0, 2)], s_near.at[1]),
        pltpu.make_async_copy(query_rope, qr, s_in.at[0]),
    ]

    def far_copy(i):
        return pltpu.make_async_copy(cache.at[listed[i]], far.at[i], s_far.at[i])

    def qa_copy(n):
        return pltpu.make_async_copy(absorbed.at[n], qa.at[n], s_qa.at[n])

    def page_copy(i):
        return pltpu.make_async_copy(cache.at[jnp.maximum(slots[i], 0)], pages.at[i], s_page.at[i])

    for c in own:
        c.start()
    for n in range(16):
        qa_copy(n).start()
        for v in range(VB):
            far_copy(n * VB + v).start()
    in_vu = pltpu.make_async_copy(value_up, vu, s_in.at[1])
    in_vu.start()

    @pl.loop(0, 48)
    def _(i):
        page_copy(i).start()

    keys[224:256] = jnp.zeros((32, 512), jnp.bfloat16)
    rope[:, 224:256] = jnp.zeros((2, 32, 128), jnp.bfloat16)
    for c in own:
        c.wait()

    def place(block, at):
        for r in range(2):
            for w in range(4):
                keys[at + 16 * r : at + 16 * r + 16, 128 * w : 128 * w + 128] = block[4 * r + w]
        first, second = rope_pair(block[8])
        for r in range(2):
            rope[0, at + 16 * r : at + 16 * r + 16] = first[r]
            rope[1, at + 16 * r : at + 16 * r + 16] = second[r]

    @pl.loop(0, 16)
    def _(n):
        qa_copy(n).wait()
        col = lax.broadcasted_iota(jnp.int32, (BLK, 256), 1)
        row = lax.broadcasted_iota(jnp.int32, (BLK, 256), 0)
        here = seq * 16 + n
        ok = (col >= 128) & (col - 128 <= SLASH * BLK + row) & (here - SLASH + (col - 128) // BLK >= 0)
        for v in range(VB):
            far_copy(n * VB + v).wait()
            place(far[n * VB + v], BLK * v)
            listed_here = listed[n * VB + v] <= here - SLASH - 1
            ok = ok | ((col // BLK == v) & listed_here)
        for v in range(SLASH + 1):
            place(near[n + v], 128 + BLK * v)
        bias = jnp.where(ok, 0.0, NEG)
        q = qa[n].reshape(512, 512)
        start = pl.multiple_of(n * BLK, BLK)
        r = jnp.concatenate([qr[pl.ds(start, BLK), 128 * p : 128 * p + 128] for p in range(HALF)], axis=0)
        s = dot_t(q, keys[...]) + jnp.concatenate([dot_t(r, rope[0]), dot_t(r, rope[1])], axis=0)
        s = (s.reshape(16, BLK, 256) + bias[None]).reshape(512, 256)
        m = jnp.max(s, axis=1, keepdims=True)
        e = jnp.exp2((s - m) * EXP2)
        total = jnp.sum(e, axis=1, keepdims=True)
        got = dot(e.astype(jnp.bfloat16), keys[...]) / total
        ctx[:, pl.ds(start, BLK), :] = got.astype(jnp.bfloat16).reshape(16, BLK, 512)
        for j in range(3):
            i = 3 * n + j
            page_copy(i).wait()
            page = pages[i]
            page = jnp.where(slots[i] >= 0, page, jnp.zeros_like(page))
            for r2 in range(2):
                rows = slice(16 * r2, 16 * r2 + 16)
                for w in range(4):
                    paged_hold[i, rows, 128 * w : 128 * w + 128] = page[4 * r2 + w]
                paged_hold[i, rows, 512:576] = page[8][:, 64 * r2 : 64 * r2 + 64]

    out_paged = pltpu.make_async_copy(paged_hold, paged.at[0], s_paged)
    out_paged.start()
    in_vu.wait()
    outs = []
    for h in range(16):
        i = even_first(h)
        cols = slice(128 * h, 128 * h + 128)
        out[:, cols] = dot(ctx[i], vu[h]).astype(jnp.bfloat16)
        got = dot(decoded[h % 2, h // 2].astype(jnp.bfloat16), vu[h]).astype(jnp.bfloat16)
        for b in range(4):
            decode_out[b, :, cols] = got[2 * b : 2 * b + 2]
        if h % 4 == 3:
            wide = slice(128 * (h - 3), 128 * h + 128)
            copy = pltpu.make_async_copy(out.at[:, wide], prefill_out.at[:, wide], s_out.at[h // 4])
            copy.start()
            outs.append(copy)
    for copy in outs:
        copy.wait()
    out_paged.wait()


def on_device(
    query_nope, query_rope, latent_cache, key_up, value_up, vertical_lists, page_owner,
    step_nope, step_rope, step_latent, prefix_lengths,
):
    seq, dec = lax.axis_index("seq"), lax.axis_index("dec")
    vmem, smem, any_ = (pl.BlockSpec(memory_space=m) for m in (pltpu.VMEM, pltpu.SMEM, pl.ANY))
    bf16, f32 = jnp.bfloat16, jnp.float32
    dma = pltpu.SemaphoreType.DMA
    cache, absorbed, decoded = pl.pallas_call(
        gather_kernel,
        out_shape=(
            jax.ShapeDtypeStruct((4, 4, 4, 2, 18, 16, 128), bf16),
            jax.ShapeDtypeStruct((16, 16, BLK, 512), bf16),
            jax.ShapeDtypeStruct((2, HALF, 8, 512), f32),
        ),
        in_specs=[smem, vmem, vmem, vmem, vmem, any_, any_],
        out_specs=(any_, any_, vmem),
        scratch_shapes=[
            pltpu.VMEM((18, 16, 128), bf16),
            pltpu.VMEM((512, 2048), bf16),
            pltpu.VMEM((16, 128, 512), bf16),
            pltpu.VMEM((2, 16, BLK, 512), bf16),
            pltpu.VMEM((2, 4, 2, 18, 16, 128), bf16),
            pltpu.VMEM((512, 512), bf16),
            pltpu.VMEM((2, 512, 128), bf16),
            pltpu.VMEM((2, HALF, 8, 512), f32),
            pltpu.VMEM((HALF, 8, 128), f32),
            pltpu.VMEM((128, 512), f32),
            pltpu.VMEM((128, 128), f32),
            pltpu.VMEM((128, 128), f32),
            dma((COPIES,)), dma((COPIES,)), dma((3,)), dma((2,)), dma((2,)),
        ],
        compiler_params=pltpu.CompilerParams(
            collective_id=0, has_side_effects=True, vmem_limit_bytes=56 << 20
        ),
        cost_estimate=pl.CostEstimate(flops=4 << 30, bytes_accessed=32 << 20, transcendentals=1 << 20),
        name="gather_absorb_decode",
    )(
        prefix_lengths, latent_cache, step_nope.reshape(8, 2048), step_rope.reshape(8, 1024),
        step_latent.reshape(8, 576), query_nope, key_up,
    )
    listed = lax.dynamic_slice(vertical_lists, (dec, seq * 16, 0), (1, 16, VB)).reshape(64)
    owned = page_owner.reshape(16, 16) == dec
    rank = jnp.cumsum(owned.astype(jnp.int32), axis=1) - 1
    picks = owned[:, None, :] & (rank[:, None, :] == jnp.arange(3)[None, :, None])
    number = jnp.arange(256).reshape(16, 1, 16)
    slots = jnp.max(jnp.where(picks, number, -1), axis=2).reshape(48)
    prefill_out, paged, decode_out = pl.pallas_call(
        attend_kernel,
        out_shape=(
            jax.ShapeDtypeStruct((512, 2048), bf16),
            jax.ShapeDtypeStruct((1, 48, BLK, 576), bf16),
            jax.ShapeDtypeStruct((4, 2, 2048), bf16),
        ),
        in_specs=[smem, smem, any_, any_, any_, any_, vmem],
        out_specs=(any_, any_, vmem),
        scratch_shapes=[
            pltpu.VMEM((18, TILES, 16, 128), bf16),
            pltpu.VMEM((64, TILES, 16, 128), bf16),
            pltpu.VMEM((16, 16, BLK, 512), bf16),
            pltpu.VMEM((512, 1024), bf16),
            pltpu.VMEM((16, 512, 128), bf16),
            pltpu.VMEM((48, TILES, 16, 128), bf16),
            pltpu.VMEM((256, 512), bf16),
            pltpu.VMEM((2, 256, 128), bf16),
            pltpu.VMEM((16, 512, 512), bf16),
            pltpu.VMEM((512, 2048), bf16),
            pltpu.VMEM((48, BLK, 576), bf16),
            dma((2,)), dma((64,)), dma((16,)), dma((2,)), dma((48,)), dma((4,)), dma,
        ],
        compiler_params=pltpu.CompilerParams(vmem_limit_bytes=56 << 20),
        cost_estimate=pl.CostEstimate(flops=6 << 30, bytes_accessed=20 << 20, transcendentals=2 << 20),
        name="attend",
    )(listed, slots, cache.reshape(256, TILES, 16, 128), absorbed, query_rope, value_up, decoded)
    return prefill_out, paged, decode_out


def solution(mesh):
    placed = (
        P("seq", "dec"), P("seq", "dec"), P(("seq", "dec"), None), P("dec", None, None), P("dec", None, None),
        P(), P(), P("seq", None, "dec"), P("seq", None, "dec"), P("seq", None, None), P("seq"),
    )
    return jax.shard_map(
        on_device,
        mesh=mesh,
        in_specs=placed,
        out_specs=(P("seq", "dec"), P("dec", None, None, None), P("seq", None, "dec")),
        check_vma=False,
    )
```

profile of v0, /device:TPU:1, one launch (start us, length us, event | category | flops | bytes accessed | tf_op | source)
XLA Modules:
  0.0 93.5 jit_solution(11734679482037629669)
XLA Ops:
  0.6 0.0 copy-start
  0.7 0.7 compare_reduce_fusion
  1.4 0.0 copy-done
  1.4 0.1 constant_dynamic-slice_fusion
  1.5 0.1 eq.32
  1.6 0.1 copy.16
  1.6 0.6 reshape.64.listed
  2.3 0.2 reduce_window_sum.11
  2.4 0.2 select_reduce_fusion
  2.6 0.1 copy.17
  2.7 0.7 reshape.68.slots
  3.3 1.3 %reshape.71.step_latent = bf16[8,576]{1,0:T(8,128)(2,1)} reshape(bf16[4,2,576]{2,1,0:T(2,128)(2,1)} %param.20) | data formatting | bytes 18432 | tf_op jit(solution)/shard_map/reshape | solution.py:461
  4.7 1.3 %reshape.70.step_rope = bf16[8,1024]{1,0:T(8,128)(2,1)} reshape(bf16[4,2,1024]{2,1,0:T(2,128)(2,1)} %param.19) | data formatting | bytes 32768 | tf_op jit(solution)/shard_map/reshape | solution.py:460
  6.0 1.4 %reshape.69.step_nope = bf16[8,2048]{1,0:T(8,128)(2,1)} reshape(bf16[4,2,2048]{2,1,0:T(2,128)(2,1)} %param.18) | data formatting | bytes 65536 | tf_op jit(solution)/shard_map/reshape | solution.py:460
  7.4 51.8 %gather_absorb_decode.1 = (bf16[4,4,4,2,18,16,128]{6,5,4,3,2,1,0:T(8,128)(2,1)}, bf16[16,16,32,512]{3,2,1,0:T(8,128)(2,1)}, f32[2,8,8,512]{3,2,1,0:T(8,128)}) custom-call(s32[4]{0:T(128)} %prefix.1, bf16[64,576]{1,0:T(8,128)(2,1)} %latent.1, bf16[8,2048]{1,0:T(8,128)(2,1)} %reshape.69.step_nope, bf16[8,1024]{1,0:T(8,128)(2,1)} %reshape.70.step_rope, ...), custom_call_target="tpu_custom_call" | custom-call | flops 4294967296 | bytes 33554432 | tf_op jit(solution)/shard_map/gather_absorb_decode/pallas_call | solution.py:430
  59.2 34.2 %attend.1 = (bf16[512,2048]{1,0:T(8,128)(2,1)}, bf16[1,48,32,576]{3,2,1,0:T(8,128)(2,1)}, bf16[4,2,2048]{2,1,0:T(2,128)(2,1)}) custom-call(s32[64]{0:T(128)} %reshape.64.listed, s32[48]{0:T(128)} %reshape.68.slots, bf16[256,9,16,128]{3,2,1,0:T(8,128)(2,1)} %bitcast.1, bf16[16,16,32,512]{3,2,1,0:T(8,128)(2,1)} %get-tuple-element.7.absorbed, ...), custom_call_target="tpu_custom_call" | custom-call | flops 6442450944 | bytes 20971520 | tf_op jit(solution)/shard_map/attend/pallas_call | solution.py:469
  (2 shorter events, 0.0 us)
Async XLA Ops:
  0.6 0.8 copy-start
where the time goes:
time: 93.9 us; the launch traced here: 93.5 us
  Pallas kernels  85.9 us (91%)
  local copies, waits for them, and re-layouts  5.7 us (6%)
  other arithmetic  1.03 us (1%)
    pallas_call x1, Pallas kernels, on_device(): pl.pallas_call(gather_kernel, out_shape=(jax.ShapeDtypeStruct((4, 4, 4, 2...  51.8 us
    pallas_call x1, Pallas kernels, on_device(): pl.pallas_call(attend_kernel, out_shape=(jax.ShapeDtypeStruct((512, 2048)...  34.2 us

commit v1 on v0

v1 whole, which is shorter than its diff:
```python
import jax
import jax.numpy as jnp
from jax import lax
from jax.experimental import pallas as pl
from jax.experimental.pallas import tpu as pltpu
from jax.sharding import PartitionSpec as P

MESH = pl.DeviceIdType.MESH
ORDERS = (("x", "y", "z"), ("y", "z", "x"), ("z", "x", "y"))
ALL = slice(None)
COPIES = 200


class Gather:
    def __init__(self, cache, send, recv):
        seq, dec = lax.axis_index("seq"), lax.axis_index("dec")
        self.at = {"x": dec // 2, "y": seq // 4, "z": seq % 4}
        self.core = dec % 2
        self.cache, self.send, self.recv = cache, send, recv
        self.own = None
        self.sent, self.number, self.shares = [], {}, []

    def device(self, axis=None, by=0, mate=False):
        at = dict(self.at)
        if axis is not None:
            at[axis] = (at[axis] + by + 4) % 4
        core = 1 - self.core if mate else self.core
        return (at["y"] * 4 + at["z"], at["x"] * 2 + core)

    def slot(self, mate=False):
        core = 1 - self.core if mate else self.core
        return self.cache.at[self.at["y"], self.at["z"], self.at["x"], core]

    def chunk(self, g, rel, mate=False):
        where = []
        for axis in ("y", "z", "x"):
            r = rel[ORDERS[g].index(axis)]
            where.append(r if isinstance(r, slice) else (self.at[axis] + r + 4) % 4)
        core = 1 - self.core if mate else self.core
        return self.cache.at[where[0], where[1], where[2], core, pl.ds(6 * g, 6)]

    def copy(self, key, src, dst, target):
        k = self.number.setdefault(key, len(self.number))
        return pltpu.make_async_remote_copy(
            src_ref=src, dst_ref=dst, send_sem=self.send.at[k], recv_sem=self.recv.at[k],
            device_id=target, device_id_type=MESH)

    def hop(self, g, phase, rel, by):
        dst = self.chunk(g, rel)
        src = self.own.at[pl.ds(6 * g, 6)] if rel == (0, 0, 0) else dst
        key = (g, phase) + tuple(map(str, rel)) + (by,)
        copy = self.copy(key, src, dst, self.device(ORDERS[g][phase], by))
        copy.start()
        self.sent.append(copy)

    def land(self, g, phase, rel, by):
        got = list(rel)
        got[phase] = {0: -by, -by: 2}[rel[phase]]
        if got[phase] == -2:
            got[phase] = 2
        dst = self.chunk(g, got)
        key = (g, phase) + tuple(map(str, rel)) + (by,)
        self.copy(key, dst, dst, self.device(mate=True)).wait_recv()
        return tuple(got)

    def give(self, g, rel):
        src = self.chunk(g, rel)
        key = ("core", g) + tuple(map(str, rel))
        copy = self.copy(key, src, src, self.device(mate=True))
        copy.start()
        self.sent.append(copy)
        self.shares.append((key, self.chunk(g, rel, mate=True)))

    def give_own(self):
        copy = self.copy(("core",), self.own, self.slot(), self.device(mate=True))
        copy.start()
        self.sent.append(copy)
        self.shares.append((("core",), self.slot(mate=True)))

    def take(self):
        for key, ref in self.shares:
            self.copy(key, ref, ref, self.device(mate=True)).wait_recv()

    def barrier_start(self):
        sem = pltpu.get_barrier_semaphore()
        for axis in ("x", "y", "z"):
            for by in (-1, 1, 2):
                pl.semaphore_signal(sem, inc=1, device_id=self.device(axis, by), device_id_type=MESH)
        pl.semaphore_signal(sem, inc=1, device_id=self.device(mate=True), device_id_type=MESH)

    def barrier_wait(self):
        pl.semaphore_wait(pltpu.get_barrier_semaphore(), 10)

    def steps(self):
        three = range(3)
        near = (1, -1)
        for phase in (0, 1):
            for g in three:
                for by in near + (2,):
                    self.hop(g, phase, (0, 0, 0), by)
        for g in three:
            for by in near:
                self.hop(g, 2, (0, 0, 0), by)
        self.give_own()
        yield "own"
        for by in near + (2,):
            for g in three:
                got = self.land(g, 0, (0, 0, 0), by)
                for way in near + (2,):
                    self.hop(g, 1, got, way)
            yield "first"
        for by in near + (2,):
            for g in three:
                got = (-by if by != 2 else 2, 0, 0)
                for way in near:
                    self.hop(g, 2, got, way)
                self.give(g, got)
        yield "first"
        for by in near + (2,):
            for g in three:
                for r1 in (0, 1, -1, 2):
                    got = self.land(g, 1, (r1, 0, 0), by)
                got = (ALL,) + got[1:]
                for way in near:
                    self.hop(g, 2, got, way)
                self.give(g, got)
            yield "second"
        for g in three:
            for r1, on in ((0, 1), (1, -1), (-1, 1), (2, -1)):
                for by in near:
                    got = self.land(g, 2, (r1, 0, 0), by)
                    if by == on:
                        self.hop(g, 2, got, by)
            for r3 in near:
                self.give(g, (ALL, 0, r3))
            yield "third"
        for r2 in near + (2,):
            for g in three:
                for by in near:
                    got = self.land(g, 2, (ALL, r2, 0), by)
                    if r2 == 2:
                        self.hop(g, 2, (slice(0, 2) if by == 1 else slice(2, 4),) + got[1:], by)
                    elif r2 == by:
                        self.hop(g, 2, got, by)
                    self.give(g, got)
                yield "third"
        for g in three:
            for r1, on in ((0, 1), (1, -1), (-1, 1), (2, -1)):
                self.land(g, 2, (r1, 0, -on), on)
            self.give(g, (ALL, 0, 2))
        yield "far"
        for r2 in near:
            for g in three:
                self.give(g, self.land(g, 2, (ALL, r2, -r2), r2))
            yield "far"
        for g in three:
            self.land(g, 2, (slice(0, 2), 2, -1), 1)
            self.land(g, 2, (slice(2, 4), 2, 1), -1)
            self.give(g, (ALL, 2, 2))
        yield "far"
        self.take()
        for copy in self.sent:
            copy.wait_send()
        yield "all"


BLK = 32
VB = 4
SLASH = 2
UNROLL = 4
EXP2 = 192.0 ** -0.5 * 1.4426950408889634
NEG = float("-inf")


def dot(a, b):
    return jnp.dot(a, b, preferred_element_type=jnp.float32)


def dot_t(a, b):
    return lax.dot_general(a, b, (((1,), (1,)), ((), ())), preferred_element_type=jnp.float32)


def pack(rows, tiles):
    for b in range(2):
        for r in range(2):
            start = 32 * b + 16 * r
            for c in range(4):
                tiles[9 * b + 4 * r + c] = rows[start : start + 16, 128 * c : 128 * c + 128]
        tiles[9 * b + 8] = jnp.concatenate(
            [rows[32 * b : 32 * b + 16, 512:576], rows[32 * b + 16 : 32 * b + 32, 512:576]], axis=1
        )


def keys_from(blocks):
    n = blocks.shape[0]

    def rows(first, second):
        return jnp.stack([first, second], axis=1).reshape(n * BLK, 128)

    latent = jnp.concatenate([rows(blocks[:, w], blocks[:, 4 + w]) for w in range(4)], axis=1)
    tile = blocks[:, 8]
    low = lax.broadcasted_iota(jnp.int32, tile.shape, 2) < 64
    zero = jnp.zeros_like(tile)
    return latent, rows(jnp.where(low, tile, zero), jnp.where(low, zero, tile))


def gather_kernel(
    prefix, latent, step_nope, step_rope, step_latent, query_nope, query_rope, key_up,
    cache, absorbed, decoded,
    tiles, qn, qr, ku, dq, acc, top, total,
    send, recv, local,
):
    t = Gather(cache, send, recv)
    t.barrier_start()
    loads = [
        pltpu.make_async_copy(src, dst, local.at[i])
        for i, (src, dst) in enumerate(((query_nope, qn), (key_up, ku), (query_rope, qr)))
    ]
    for c in loads:
        c.start()
    pack(latent, tiles)
    t.own = tiles
    t.barrier_wait()
    own_copy = pltpu.make_async_copy(tiles, t.slot(), local.at[3])
    own_copy.start()

    def absorb(h):
        got = dot(qn[:, 128 * h : 128 * h + 128], ku[h]).astype(jnp.bfloat16)
        absorbed[:, h, :, :512] = got.reshape(16, BLK, 512)
        rope = qr[:, 64 * h : 64 * h + 64]
        absorbed[:, h, :, 512:] = jnp.concatenate([rope, rope], axis=1).reshape(16, BLK, 128)

    def decode_start():
        for h in range(16):
            dq[h, :, :512] = dot(step_nope[:, 128 * h : 128 * h + 128], ku[h])
            rope = step_rope[:, 64 * h : 64 * h + 64].astype(jnp.float32)
            dq[h, :, 512:] = jnp.concatenate([rope, rope], axis=1)
        q = dq[...].reshape(128, 640).astype(jnp.bfloat16)
        fresh = step_latent[...]
        s = dot_t(q[:, :576], fresh)
        row = lax.broadcasted_iota(jnp.int32, (128, 8), 0) % 8
        key = lax.broadcasted_iota(jnp.int32, (128, 8), 1)
        s = jnp.where((row // 2 == key // 2) & (key <= row), s, NEG)
        m = jnp.max(s, axis=1, keepdims=True)
        e = jnp.exp2((s - m) * EXP2)
        top[...] = jnp.broadcast_to(m, (128, 128))
        total[...] = jnp.broadcast_to(jnp.sum(e, axis=1, keepdims=True), (128, 128))
        acc[...] = dot(e.astype(jnp.bfloat16), fresh[:, :512])

    def decode(n):
        values, rope = keys_from(cache[n // 4, n % 4].reshape(16, 9, 16, 128))
        q = dq[...].reshape(128, 640).astype(jnp.bfloat16)
        s = dot_t(q, jnp.concatenate([values, rope], axis=1))
        row = lax.broadcasted_iota(jnp.int32, (128, 512), 0) % 8 // 2
        limit = jnp.where(row == 0, prefix[0], jnp.where(row == 1, prefix[1], jnp.where(row == 2, prefix[2], prefix[3])))
        place = lax.broadcasted_iota(jnp.int32, (128, 512), 1) + 512 * n
        s = jnp.where(place < limit, s, NEG)
        before = top[:, :1]
        m = jnp.maximum(before, jnp.max(s, axis=1, keepdims=True))
        keep = jnp.exp2((before - m) * EXP2)
        e = jnp.exp2((s - m) * EXP2)
        top[...] = jnp.broadcast_to(m, (128, 128))
        total[...] = total[...] * keep + jnp.sum(e, axis=1, keepdims=True)
        acc[...] = acc[...] * keep + dot(e.astype(jnp.bfloat16), values)

    step = 0
    for name in t.steps():
        if step == 0:
            for c in loads:
                c.wait()
        if step < 8:
            absorb(2 * step)
            absorb(2 * step + 1)
        elif step == 8:
            decode_start()
        step += 1
    own_copy.wait()
    for n in range(16):
        decode(n)
    decoded[...] = (acc[...] / total[:, :1]).reshape(16, 8, 512)


def attend_kernel(
    listed, slots, cache, absorbed, value_up, decoded,
    prefill_out, paged, decode_out,
    vu, ctx, out, paged_hold,
    s_in, s_out, s_paged,
):
    seq = lax.axis_index("seq")
    in_vu = pltpu.make_async_copy(value_up, vu, s_in)
    in_vu.start()

    def block(i):
        return cache[i // 64, i // 16 % 4, i // 4 % 4, i // 2 % 2, pl.ds(i % 2 * 9, 9)][None]

    def keys_of(n):
        here = seq * 16 + n
        blocks = [block(listed[n * VB + v]) for v in range(VB)]
        blocks += [block(jnp.maximum(here - SLASH + v, 0)) for v in range(SLASH + 1)]
        blocks.append(jnp.zeros((1, 9, 16, 128), jnp.bfloat16))
        return keys_from(jnp.concatenate(blocks, axis=0))

    col = lax.broadcasted_iota(jnp.int32, (BLK, 256), 1)
    row = lax.broadcasted_iota(jnp.int32, (BLK, 256), 0)
    causal = (col >= 128) & (col - 128 <= SLASH * BLK + row)

    def score(n):
        here = seq * 16 + n
        ok = causal & (here - SLASH + (col - 128) // BLK >= 0)
        for v in range(VB):
            ok = ok | ((col // BLK == v) & (listed[n * VB + v] <= here - SLASH - 1))
        bias = jnp.where(ok, 0.0, NEG)
        values, rope = keys_of(n)
        s = dot_t(absorbed[n].reshape(512, 640), jnp.concatenate([values, rope], axis=1))
        return (s.reshape(16, BLK, 256) + bias[None]).reshape(512, 256)

    def weigh(s):
        m = jnp.max(s, axis=1, keepdims=True)
        e = jnp.exp2((s - m) * EXP2)
        return e.astype(jnp.bfloat16), 1.0 / jnp.sum(e, axis=1, keepdims=True)

    def mix(n, e, inverse):
        got = dot(e, keys_of(n)[0]) * inverse
        start = pl.multiple_of(n * BLK, BLK)
        ctx[:, pl.ds(start, BLK), :] = got.astype(jnp.bfloat16).reshape(16, BLK, 512)

    shift = (
        lax.broadcasted_iota(jnp.int32, (128, 128), 0) == lax.broadcasted_iota(jnp.int32, (128, 128), 1) + 64
    ).astype(jnp.float32).astype(jnp.bfloat16)
    group = 3 * UNROLL

    def pages_out(k):
        ropes = []
        for j in range(group):
            i = k * group + j
            page = block(jnp.maximum(slots[i], 0))[0]
            page = jnp.where(slots[i] >= 0, page, jnp.zeros_like(page))
            for r in range(2):
                for w in range(4):
                    paged_hold[i, 16 * r : 16 * r + 16, 128 * w : 128 * w + 128] = page[4 * r + w]
            ropes.append(page[8])
        second = dot(jnp.concatenate(ropes, axis=0), shift).astype(jnp.bfloat16)
        for j in range(group):
            i = k * group + j
            paged_hold[i, :16, 512:576] = ropes[j][:, :64]
            paged_hold[i, 16:, 512:576] = second[16 * j : 16 * j + 16, :64]
        pages_copy(k).start()

    def pages_copy(k):
        part = pl.ds(k * group, group)
        return pltpu.make_async_copy(paged_hold.at[part], paged.at[0, part], s_paged.at[k])

    @pl.loop(0, 16 // UNROLL)
    def _(k):
        turns = [k * UNROLL + u for u in range(UNROLL)]
        scores = [score(n) for n in turns]
        weights = [weigh(s) for s in scores]
        for n, w in zip(turns, weights):
            mix(n, *w)
        pages_out(k)

    in_vu.wait()
    outs = []
    for h in range(16):
        cols = slice(128 * h, 128 * h + 128)
        out[:, cols] = dot(ctx[h], vu[h]).astype(jnp.bfloat16)
        got = dot(decoded[h].astype(jnp.bfloat16), vu[h]).astype(jnp.bfloat16)
        for b in range(4):
            decode_out[b, :, cols] = got[2 * b : 2 * b + 2]
        if h % 4 == 3:
            wide = slice(128 * (h - 3), 128 * h + 128)
            copy = pltpu.make_async_copy(out.at[:, wide], prefill_out.at[:, wide], s_out.at[h // 4])
            copy.start()
            outs.append(copy)
    for copy in outs:
        copy.wait()
    for k in range(16 // UNROLL):
        pages_copy(k).wait()


def gather_call(prefix_lengths, latent_cache, step_nope, step_rope, step_latent, query_nope, query_rope, key_up):
    vmem, smem, any_ = (pl.BlockSpec(memory_space=m) for m in (pltpu.VMEM, pltpu.SMEM, pl.ANY))
    bf16, f32 = jnp.bfloat16, jnp.float32
    dma = pltpu.SemaphoreType.DMA
    query_nope, query_rope, key_up = (
        pltpu.with_memory_space_constraint(x, pltpu.HBM) for x in (query_nope, query_rope, key_up)
    )
    return pl.pallas_call(
        gather_kernel,
        out_shape=(
            pltpu.VMEM((4, 4, 4, 2, 18, 16, 128), bf16),
            pltpu.VMEM((16, 16, BLK, 640), bf16),
            pltpu.VMEM((16, 8, 512), f32),
        ),
        in_specs=[smem, vmem, vmem, vmem, vmem, any_, any_, any_],
        out_specs=(vmem, vmem, vmem),
        scratch_shapes=[
            pltpu.VMEM((18, 16, 128), bf16),
            pltpu.VMEM((512, 2048), bf16),
            pltpu.VMEM((512, 1024), bf16),
            pltpu.VMEM((16, 128, 512), bf16),
            pltpu.VMEM((16, 8, 640), f32),
            pltpu.VMEM((128, 512), f32),
            pltpu.VMEM((128, 128), f32),
            pltpu.VMEM((128, 128), f32),
            dma((COPIES,)), dma((COPIES,)), dma((4,)),
        ],
        compiler_params=pltpu.CompilerParams(
            collective_id=0, has_side_effects=True, vmem_limit_bytes=16 << 20
        ),
        cost_estimate=pl.CostEstimate(flops=4 << 30, bytes_accessed=32 << 20, transcendentals=1 << 20),
        name="gather_absorb_decode",
    )(prefix_lengths, latent_cache, step_nope, step_rope, step_latent, query_nope, query_rope, key_up)


def attend_call(listed, slots, cache, absorbed, value_up, decoded):
    vmem, smem, any_ = (pl.BlockSpec(memory_space=m) for m in (pltpu.VMEM, pltpu.SMEM, pl.ANY))
    bf16 = jnp.bfloat16
    dma = pltpu.SemaphoreType.DMA
    cache, absorbed, decoded = (
        pltpu.with_memory_space_constraint(x, pltpu.VMEM) for x in (cache, absorbed, decoded)
    )
    value_up = pltpu.with_memory_space_constraint(value_up, pltpu.HBM)
    return pl.pallas_call(
        attend_kernel,
        out_shape=(
            jax.ShapeDtypeStruct((512, 2048), bf16),
            jax.ShapeDtypeStruct((1, 48, BLK, 576), bf16),
            jax.ShapeDtypeStruct((4, 2, 2048), bf16),
        ),
        in_specs=[smem, smem, vmem, vmem, any_, vmem],
        out_specs=(any_, any_, vmem),
        scratch_shapes=[
            pltpu.VMEM((16, 512, 128), bf16),
            pltpu.VMEM((16, 512, 512), bf16),
            pltpu.VMEM((512, 2048), bf16),
            pltpu.VMEM((48, BLK, 576), bf16),
            dma, dma((4,)), dma((4,)),
        ],
        compiler_params=pltpu.CompilerParams(vmem_limit_bytes=20 << 20),
        cost_estimate=pl.CostEstimate(flops=6 << 30, bytes_accessed=20 << 20, transcendentals=2 << 20),
        name="attend",
    )(listed, slots, cache, absorbed, value_up, decoded)


def on_device(
    query_nope, query_rope, latent_cache, key_up, value_up, vertical_lists, page_owner,
    step_nope, step_rope, step_latent, prefix_lengths,
):
    seq, dec = lax.axis_index("seq"), lax.axis_index("dec")
    cache, absorbed, decoded = gather_call(
        prefix_lengths, latent_cache, step_nope.reshape(8, 2048), step_rope.reshape(8, 1024),
        step_latent.reshape(8, 576), query_nope, query_rope, key_up,
    )
    listed = lax.dynamic_slice(vertical_lists, (dec, seq * 16, 0), (1, 16, VB)).reshape(64)
    owned = page_owner.reshape(16, 16) == dec
    rank = jnp.cumsum(owned.astype(jnp.int32), axis=1) - 1
    picks = owned[:, None, :] & (rank[:, None, :] == jnp.arange(3)[None, :, None])
    number = jnp.arange(256).reshape(16, 1, 16)
    slots = jnp.max(jnp.where(picks, number, -1), axis=2).reshape(48)
    return attend_call(listed, slots, cache, absorbed, value_up, decoded)


def solution(mesh):
    placed = (
        P("seq", "dec"), P("seq", "dec"), P(("seq", "dec"), None), P("dec", None, None), P("dec", None, None),
        P(), P(), P("seq", None, "dec"), P("seq", None, "dec"), P("seq", None, None), P("seq"),
    )
    return jax.shard_map(
        on_device,
        mesh=mesh,
        in_specs=placed,
        out_specs=(P("seq", "dec"), P("dec", None, None, None), P("seq", None, "dec")),
        check_vma=False,
    )
```

time: 93.9 us -> 65 us (0.69)
  Pallas kernels: 85.9 us -> 58.4 us
  local copies, waits for them, and re-layouts: 5.7 us -> 4.33 us
    pallas_call x2, Pallas kernels: 85.9 us -> 58.4 us  [the longest x1 44.3 us: gather_call(): pl.pallas_call(gather_kernel, out_shape=(pltpu.VMEM((4, 4, 4, 2, 18, 16,...]
    unnamed x2 -> x6, local copies, waits for them, and re-layouts: 0.05 us -> 1.59 us
where the time goes in v1:
time: 65 us; the launch traced here: 64.7 us
  Pallas kernels  58.4 us (90%)
  local copies, waits for them, and re-layouts  4.33 us (7%)
  other arithmetic  1.03 us (2%)
  between operations  0.84 us (1%)
    pallas_call x1, Pallas kernels, gather_call(): pl.pallas_call(gather_kernel, out_shape=(pltpu.VMEM((4, 4, 4, 2, 18, 16,...  44.3 us
    pallas_call x1, Pallas kernels, attend_call(): pl.pallas_call(attend_kernel, out_shape=(jax.ShapeDtypeStruct((512, 2048)...  14.2 us
    unnamed x6, local copies, waits for them, and re-layouts  1.59 us

profile of v1, /device:TPU:1, one launch (start us, length us, event | category | flops | bytes accessed | tf_op | source)
XLA Modules:
  0.0 64.7 jit_solution(12901043403037961173)
XLA Ops:
  0.6 0.0 copy-start
  0.7 0.7 %compare_reduce_fusion = pred[256]{0:T(512)(128)(4,1)S(1)} fusion(s32[256,1]{0,1:T(1,128)} %param.17, s32[]{:T(128)S(6)} %axis_index.22), kind=kLoop, calls=%fused_computation.5 | loop fusion | flops 256 | bytes 1284 | tf_op jit(solution)/shard_map/eq | solution.py:456
  1.4 0.0 copy-done
  1.4 0.1 constant_dynamic-slice_fusion
  1.5 0.1 eq.32
  1.6 0.1 copy.16
  1.6 0.1 reshape.61.listed
  1.7 0.2 reduce_window_sum.11
  1.9 0.2 select_reduce_fusion
  2.1 0.1 copy.17
  2.2 0.1 reshape.65.slots
  2.3 0.7 %reshape.68.step_latent = bf16[8,576]{1,0:T(8,128)(2,1)S(1)} reshape(bf16[4,2,576]{2,1,0:T(2,128)(2,1)} %param.20) | data formatting | bytes 18432 | tf_op jit(solution)/shard_map/reshape | solution.py:453
  3.0 0.7 %reshape.67.step_rope = bf16[8,1024]{1,0:T(8,128)(2,1)S(1)} reshape(bf16[4,2,1024]{2,1,0:T(2,128)(2,1)} %param.19) | data formatting | bytes 32768 | tf_op jit(solution)/shard_map/reshape | solution.py:452
  3.7 0.8 %reshape.66.step_nope = bf16[8,2048]{1,0:T(8,128)(2,1)S(1)} reshape(bf16[4,2,2048]{2,1,0:T(2,128)(2,1)} %param.18) | data formatting | bytes 65536 | tf_op jit(solution)/shard_map/reshape | solution.py:452
  4.5 0.0 copy-start.1
  4.5 0.9 %copy-done.1 = bf16[64,576]{1,0:T(8,128)(2,1)S(1)} copy-done((bf16[64,576]{1,0:T(8,128)(2,1)S(1)}, bf16[64,576]{1,0:T(8,128)(2,1)}, u32[]{:S(2)}) %copy-start.1) | copy-done | bytes 73752
  5.4 0.0 copy-start.2
  5.4 0.7 %copy-done.2 = s32[4]{0:T(128)S(1)} copy-done((s32[4]{0:T(128)S(1)}, s32[4]{0:T(128)}, u32[]{:S(2)}) %copy-start.2) | copy-done | bytes 40
  6.0 44.3 %gather_absorb_decode.1 = (bf16[4,4,4,2,18,16,128]{6,5,4,3,2,1,0:T(8,128)(2,1)S(1)}, bf16[16,16,32,640]{3,2,1,0:T(8,128)(2,1)S(1)}, f32[16,8,512]{2,1,0:T(8,128)S(1)}) custom-call(s32[4]{0:T(128)S(1)} %copy-done.2, bf16[64,576]{1,0:T(8,128)(2,1)S(1)} %copy-done.1, bf16[8,2048]{1,0:T(8,128)(2,1)S(1)} %reshape.66.step_nope, ...), custom_call_target="tpu_custom_call" | custom-call | flops 4294967296 | bytes 33554432 | tf_op jit(solution)/shard_map/gather_absorb_decode/pallas_call | solution.py:388
  50.3 14.2 %attend.1 = (bf16[512,2048]{1,0:T(8,128)(2,1)}, bf16[1,48,32,576]{3,2,1,0:T(8,128)(2,1)}, bf16[4,2,2048]{2,1,0:T(2,128)(2,1)}) custom-call(s32[64]{0:T(128)S(1)} %reshape.61.listed, s32[48]{0:T(128)S(1)} %reshape.65.slots, bf16[4,4,4,2,18,16,128]{6,5,4,3,2,1,0:T(8,128)(2,1)S(1)} %get-tuple-element.6.cache, ...), custom_call_target="tpu_custom_call" | custom-call | flops 6442450944 | bytes 20971520 | tf_op jit(solution)/shard_map/attend/pallas_call | solution.py:424
  (2 shorter events, 0.0 us)
Async XLA Ops:
  0.6 0.8 %copy-start = (s32[8,256,4]{1,2,0:T(4,128)S(1)}, s32[8,256,4]{1,2,0:T(4,128)}, u32[]{:S(2)}) copy-start(s32[8,256,4]{1,2,0:T(4,128)} %param.16) | copy-start | bytes 98308
  4.5 0.9 %copy-start.1 = (bf16[64,576]{1,0:T(8,128)(2,1)S(1)}, bf16[64,576]{1,0:T(8,128)(2,1)}, u32[]{:S(2)}) copy-start(bf16[64,576]{1,0:T(8,128)(2,1)} %latent.1) | copy-start | bytes 221188
  5.4 0.7 %copy-start.2 = (s32[4]{0:T(128)S(1)}, s32[4]{0:T(128)}, u32[]{:S(2)}) copy-start(s32[4]{0:T(128)} %prefix.1) | copy-start | bytes 52

commit v2 on v1

--- a/solution.py
+++ b/solution.py
@@ -18,7 +18,7 @@
         self.core = dec % 2
         self.cache, self.send, self.recv = cache, send, recv
         self.own = None
-        self.sent, self.number, self.shares = [], {}, []
+        self.sent, self.number, self.shares = [], {}, {}
 
     def device(self, axis=None, by=0, mate=False):
         at = dict(self.at)
@@ -30,6 +30,9 @@
     def slot(self, mate=False):
         core = 1 - self.core if mate else self.core
         return self.cache.at[self.at["y"], self.at["z"], self.at["x"], core]
+
+    def spot(self, axis, by):
+        return (self.at[axis] + by + 4) % 4
 
     def chunk(self, g, rel, mate=False):
         where = []
@@ -69,17 +72,31 @@
         copy = self.copy(key, src, src, self.device(mate=True))
         copy.start()
         self.sent.append(copy)
-        self.shares.append((key, self.chunk(g, rel, mate=True)))
+        self.shares[key] = self.chunk(g, rel, mate=True)
 
     def give_own(self):
         copy = self.copy(("core",), self.own, self.slot(), self.device(mate=True))
         copy.start()
         self.sent.append(copy)
-        self.shares.append((("core",), self.slot(mate=True)))
-
-    def take(self):
-        for key, ref in self.shares:
+        self.shares[("core",)] = self.slot(mate=True)
+
+    def wait_share(self, key):
+        ref = self.shares.pop(key, None)
+        if ref is not None:
             self.copy(key, ref, ref, self.device(mate=True)).wait_recv()
+
+    def take(self, place):
+        for g in range(3):
+            rel = tuple(place[axis] for axis in ORDERS[g])
+            if rel[1:] != (0, 0):
+                rel = (ALL,) + rel[1:]
+            self.wait_share(("core",) + (() if rel == (0, 0, 0) else (g,) + tuple(map(str, rel))))
+
+    def finish(self):
+        for key in list(self.shares):
+            self.wait_share(key)
+        for copy in self.sent:
+            copy.wait_send()
 
     def barrier_start(self):
         sem = pltpu.get_barrier_semaphore()
@@ -134,6 +151,7 @@
             for r3 in near:
                 self.give(g, (ALL, 0, r3))
             yield "third"
+        yield (0, 1)
         for r2 in near + (2,):
             for g in three:
                 for by in near:
@@ -144,30 +162,41 @@
                         self.hop(g, 2, got, by)
                     self.give(g, got)
                 yield "third"
+            yield (r2, 1)
         for g in three:
             for r1, on in ((0, 1), (1, -1), (-1, 1), (2, -1)):
                 self.land(g, 2, (r1, 0, -on), on)
             self.give(g, (ALL, 0, 2))
-        yield "far"
+        yield (0, 2)
         for r2 in near:
             for g in three:
                 self.give(g, self.land(g, 2, (ALL, r2, -r2), r2))
-            yield "far"
+            yield (r2, 2)
         for g in three:
             self.land(g, 2, (slice(0, 2), 2, -1), 1)
             self.land(g, 2, (slice(2, 4), 2, 1), -1)
             self.give(g, (ALL, 2, 2))
-        yield "far"
-        self.take()
-        for copy in self.sent:
-            copy.wait_send()
-        yield "all"
+        yield (2, 2)
+
+
+MARKS = [(0, 1), (1, 1), (-1, 1), (2, 1), (0, 2), (1, 2), (-1, 2), (2, 2)]
+
+
+def complete_at(place):
+    last = 0
+    for order in ORDERS:
+        second, third = place[order[1]], place[order[2]]
+        if third:
+            last = max(last, MARKS.index((second, 2 if third == 2 else 1)))
+    return last
 
 
 BLK = 32
 VB = 4
 SLASH = 2
 UNROLL = 4
+QUANTA = 1
+REL = (0, 1, -1, 2)
 EXP2 = 192.0 ** -0.5 * 1.4426950408889634
 NEG = float("-inf")
 
@@ -205,24 +234,49 @@
 
 
 def gather_kernel(
-    prefix, latent, step_nope, step_rope, step_latent, query_nope, query_rope, key_up,
-    cache, absorbed, decoded,
-    tiles, qn, qr, ku, dq, acc, top, total,
+    prefix_in, latent_in, lists_in, owner_in, nope_in, rope_in, fresh_in, query_nope, query_rope, key_up,
+    cache, absorbed, decoded, listed, slots,
+    prefix, latent, owner, step_nope, step_rope, step_latent, tiles, qn, qr, ku, sn, sl, dq, acc, top, total, slot_rows,
     send, recv, local,
 ):
     t = Gather(cache, send, recv)
     t.barrier_start()
+    first = pltpu.make_async_copy(latent_in, latent, local.at[9])
+    first.start()
+    dec = lax.axis_index("dec")
     loads = [
         pltpu.make_async_copy(src, dst, local.at[i])
-        for i, (src, dst) in enumerate(((query_nope, qn), (key_up, ku), (query_rope, qr)))
+        for i, (src, dst) in enumerate(
+            (
+                (query_nope, qn), (key_up, ku), (query_rope, qr), (prefix_in, prefix), (lists_in.at[dec], listed),
+                (owner_in, owner), (nope_in, step_nope), (rope_in, step_rope), (fresh_in, step_latent),
+            )
+        )
     ]
     for c in loads:
         c.start()
+    first.wait()
     pack(latent, tiles)
     t.own = tiles
     t.barrier_wait()
-    own_copy = pltpu.make_async_copy(tiles, t.slot(), local.at[3])
+    own_copy = pltpu.make_async_copy(tiles, t.slot(), local.at[10])
     own_copy.start()
+
+    def page_slots():
+        page = lax.broadcasted_iota(jnp.int32, (256, 256), 0)
+        other = lax.broadcasted_iota(jnp.int32, (256, 256), 1)
+        before = ((page // 16 == other // 16) & (page < other)).astype(jnp.float32).astype(jnp.bfloat16)
+        owned = jnp.broadcast_to((owner[...] == dec).astype(jnp.float32), (8, 256))
+        rank = dot(owned.astype(jnp.bfloat16), before)
+        turn = lax.broadcasted_iota(jnp.int32, (8, 256), 0).astype(jnp.float32)
+        pick = jnp.where((owned > 0) & (rank == turn), 1.0, 0.0)
+        number = lax.broadcasted_iota(jnp.int32, (8, 256), 1).astype(jnp.float32)
+        home = (
+            lax.broadcasted_iota(jnp.int32, (256, 128), 0) // 16 == lax.broadcasted_iota(jnp.int32, (256, 128), 1)
+        ).astype(jnp.float32).astype(jnp.bfloat16)
+        which = dot((pick * number).astype(jnp.bfloat16), home)
+        some = dot(pick.astype(jnp.bfloat16), home)
+        slot_rows[...] = jnp.where(some > 0, which, -1.0).astype(jnp.int32)
 
     def absorb(h):
         got = dot(qn[:, 128 * h : 128 * h + 128], ku[h]).astype(jnp.bfloat16)
@@ -231,12 +285,16 @@
         absorbed[:, h, :, 512:] = jnp.concatenate([rope, rope], axis=1).reshape(16, BLK, 128)
 
     def decode_start():
+        for b in range(4):
+            sn[2 * b : 2 * b + 2, :2048] = step_nope[b].astype(jnp.float32)
+            sn[2 * b : 2 * b + 2, 2048:] = step_rope[b].astype(jnp.float32)
+            sl[2 * b : 2 * b + 2] = step_latent[b].astype(jnp.float32)
         for h in range(16):
-            dq[h, :, :512] = dot(step_nope[:, 128 * h : 128 * h + 128], ku[h])
-            rope = step_rope[:, 64 * h : 64 * h + 64].astype(jnp.float32)
+            dq[h, :, :512] = dot(sn[:, 128 * h : 128 * h + 128].astype(jnp.bfloat16), ku[h])
+            rope = sn[:, 2048 + 64 * h : 2048 + 64 * h + 64]
             dq[h, :, 512:] = jnp.concatenate([rope, rope], axis=1)
         q = dq[...].reshape(128, 640).astype(jnp.bfloat16)
-        fresh = step_latent[...]
+        fresh = sl[...].astype(jnp.bfloat16)
         s = dot_t(q[:, :576], fresh)
         row = lax.broadcasted_iota(jnp.int32, (128, 8), 0) % 8
         key = lax.broadcasted_iota(jnp.int32, (128, 8), 1)
@@ -247,13 +305,20 @@
         total[...] = jnp.broadcast_to(jnp.sum(e, axis=1, keepdims=True), (128, 128))
         acc[...] = dot(e.astype(jnp.bfloat16), fresh[:, :512])
 
-    def decode(n):
-        values, rope = keys_from(cache[n // 4, n % 4].reshape(16, 9, 16, 128))
+    def decode(places):
+        n = 128 * len(places)
+        blocks, homes = [], []
+        for place in places:
+            t.take(place)
+            y, z, x = (t.spot(axis, place[axis]) for axis in ("y", "z", "x"))
+            blocks.append(cache[y, z, x].reshape(4, 9, 16, 128))
+            homes.append(lax.broadcasted_iota(jnp.int32, (128, 128), 1) + 128 * (16 * y + 4 * z + x))
+        values, rope = keys_from(jnp.concatenate(blocks, axis=0))
         q = dq[...].reshape(128, 640).astype(jnp.bfloat16)
         s = dot_t(q, jnp.concatenate([values, rope], axis=1))
-        row = lax.broadcasted_iota(jnp.int32, (128, 512), 0) % 8 // 2
+        row = lax.broadcasted_iota(jnp.int32, (128, n), 0) % 8 // 2
         limit = jnp.where(row == 0, prefix[0], jnp.where(row == 1, prefix[1], jnp.where(row == 2, prefix[2], prefix[3])))
-        place = lax.broadcasted_iota(jnp.int32, (128, 512), 1) + 512 * n
+        place = jnp.concatenate(homes, axis=1)
         s = jnp.where(place < limit, s, NEG)
         before = top[:, :1]
         m = jnp.maximum(before, jnp.max(s, axis=1, keepdims=True))
@@ -263,20 +328,39 @@
         total[...] = total[...] * keep + jnp.sum(e, axis=1, keepdims=True)
         acc[...] = acc[...] * keep + dot(e.astype(jnp.bfloat16), values)
 
+    waiting = [dict(x=x, y=y, z=z) for x in REL for y in REL for z in REL]
+    waiting.sort(key=complete_at)
+    here = -1
+
+    def decode_some(most, all_of=False):
+        for _ in range(most):
+            ready = [p for p in waiting if complete_at(p) <= here]
+            if len(ready) >= 4 or (all_of and ready):
+                decode(ready[:4])
+                del waiting[: len(ready[:4])]
+
     step = 0
-    for name in t.steps():
+    for mark in t.steps():
         if step == 0:
             for c in loads:
                 c.wait()
+            page_slots()
+            out_slots = pltpu.make_async_copy(slot_rows, slots, local.at[11])
+            out_slots.start()
         if step < 8:
             absorb(2 * step)
             absorb(2 * step + 1)
         elif step == 8:
             decode_start()
+            own_copy.wait()
+        if mark in MARKS:
+            here = MARKS.index(mark)
+        if here >= 0:
+            decode_some(QUANTA)
         step += 1
-    own_copy.wait()
-    for n in range(16):
-        decode(n)
+    decode_some(64, True)
+    t.finish()
+    out_slots.wait()
     decoded[...] = (acc[...] / total[:, :1]).reshape(16, 8, 512)
 
 
@@ -295,7 +379,7 @@
 
     def keys_of(n):
         here = seq * 16 + n
-        blocks = [block(listed[n * VB + v]) for v in range(VB)]
+        blocks = [block(listed[v, here]) for v in range(VB)]
         blocks += [block(jnp.maximum(here - SLASH + v, 0)) for v in range(SLASH + 1)]
         blocks.append(jnp.zeros((1, 9, 16, 128), jnp.bfloat16))
         return keys_from(jnp.concatenate(blocks, axis=0))
@@ -308,7 +392,7 @@
         here = seq * 16 + n
         ok = causal & (here - SLASH + (col - 128) // BLK >= 0)
         for v in range(VB):
-            ok = ok | ((col // BLK == v) & (listed[n * VB + v] <= here - SLASH - 1))
+            ok = ok | ((col // BLK == v) & (listed[v, here] <= here - SLASH - 1))
         bias = jnp.where(ok, 0.0, NEG)
         values, rope = keys_of(n)
         s = dot_t(absorbed[n].reshape(512, 640), jnp.concatenate([values, rope], axis=1))
@@ -333,8 +417,9 @@
         ropes = []
         for j in range(group):
             i = k * group + j
-            page = block(jnp.maximum(slots[i], 0))[0]
-            page = jnp.where(slots[i] >= 0, page, jnp.zeros_like(page))
+            which = slots[j % 3, k * UNROLL + j // 3]
+            page = block(jnp.maximum(which, 0))[0]
+            page = jnp.where(which >= 0, page, jnp.zeros_like(page))
             for r in range(2):
                 for w in range(4):
                     paged_hold[i, 16 * r : 16 * r + 16, 128 * w : 128 * w + 128] = page[4 * r + w]
@@ -378,39 +463,49 @@
         pages_copy(k).wait()
 
 
-def gather_call(prefix_lengths, latent_cache, step_nope, step_rope, step_latent, query_nope, query_rope, key_up):
-    vmem, smem, any_ = (pl.BlockSpec(memory_space=m) for m in (pltpu.VMEM, pltpu.SMEM, pl.ANY))
-    bf16, f32 = jnp.bfloat16, jnp.float32
+def gather_call(*args):
+    vmem, any_ = pl.BlockSpec(memory_space=pltpu.VMEM), pl.BlockSpec(memory_space=pl.ANY)
+    smem = pl.BlockSpec(memory_space=pltpu.SMEM)
+    bf16, f32, i32 = jnp.bfloat16, jnp.float32, jnp.int32
     dma = pltpu.SemaphoreType.DMA
-    query_nope, query_rope, key_up = (
-        pltpu.with_memory_space_constraint(x, pltpu.HBM) for x in (query_nope, query_rope, key_up)
-    )
+    args = [pltpu.with_memory_space_constraint(x, pltpu.HBM) for x in args]
     return pl.pallas_call(
         gather_kernel,
         out_shape=(
             pltpu.VMEM((4, 4, 4, 2, 18, 16, 128), bf16),
             pltpu.VMEM((16, 16, BLK, 640), bf16),
             pltpu.VMEM((16, 8, 512), f32),
+            pltpu.SMEM((4, 256), i32),
+            pltpu.SMEM((8, 128), i32),
         ),
-        in_specs=[smem, vmem, vmem, vmem, vmem, any_, any_, any_],
-        out_specs=(vmem, vmem, vmem),
+        in_specs=[any_] * 10,
+        out_specs=(vmem, vmem, vmem, smem, smem),
         scratch_shapes=[
+            pltpu.SMEM((4,), i32),
+            pltpu.VMEM((64, 576), bf16),
+            pltpu.VMEM((1, 256), i32),
+            pltpu.VMEM((4, 2, 2048), bf16),
+            pltpu.VMEM((4, 2, 1024), bf16),
+            pltpu.VMEM((4, 2, 576), bf16),
             pltpu.VMEM((18, 16, 128), bf16),
             pltpu.VMEM((512, 2048), bf16),
             pltpu.VMEM((512, 1024), bf16),
             pltpu.VMEM((16, 128, 512), bf16),
+            pltpu.VMEM((8, 3072), f32),
+            pltpu.VMEM((8, 576), f32),
             pltpu.VMEM((16, 8, 640), f32),
             pltpu.VMEM((128, 512), f32),
             pltpu.VMEM((128, 128), f32),
             pltpu.VMEM((128, 128), f32),
-            dma((COPIES,)), dma((COPIES,)), dma((4,)),
+            pltpu.VMEM((8, 128), i32),
+            dma((COPIES,)), dma((COPIES,)), dma((12,)),
         ],
         compiler_params=pltpu.CompilerParams(
             collective_id=0, has_side_effects=True, vmem_limit_bytes=16 << 20
         ),
         cost_estimate=pl.CostEstimate(flops=4 << 30, bytes_accessed=32 << 20, transcendentals=1 << 20),
         name="gather_absorb_decode",
-    )(prefix_lengths, latent_cache, step_nope, step_rope, step_latent, query_nope, query_rope, key_up)
+    )(*args)
 
 
 def attend_call(listed, slots, cache, absorbed, value_up, decoded):
@@ -420,6 +515,7 @@
     cache, absorbed, decoded = (
         pltpu.with_memory_space_constraint(x, pltpu.VMEM) for x in (cache, absorbed, decoded)
     )
+    listed, slots = (pltpu.with_memory_space_constraint(x, pltpu.SMEM) for x in (listed, slots))
     value_up = pltpu.with_memory_space_constraint(value_up, pltpu.HBM)
     return pl.pallas_call(
         attend_kernel,
@@ -447,17 +543,10 @@
     query_nope, query_rope, latent_cache, key_up, value_up, vertical_lists, page_owner,
     step_nope, step_rope, step_latent, prefix_lengths,
 ):
-    seq, dec = lax.axis_index("seq"), lax.axis_index("dec")
-    cache, absorbed, decoded = gather_call(
-        prefix_lengths, latent_cache, step_nope.reshape(8, 2048), step_rope.reshape(8, 1024),
-        step_latent.reshape(8, 576), query_nope, query_rope, key_up,
+    cache, absorbed, decoded, listed, slots = gather_call(
+        prefix_lengths, latent_cache, vertical_lists.transpose(0, 2, 1), page_owner.reshape(1, 256),
+        step_nope, step_rope, step_latent, query_nope, query_rope, key_up,
     )
-    listed = lax.dynamic_slice(vertical_lists, (dec, seq * 16, 0), (1, 16, VB)).reshape(64)
-    owned = page_owner.reshape(16, 16) == dec
-    rank = jnp.cumsum(owned.astype(jnp.int32), axis=1) - 1
-    picks = owned[:, None, :] & (rank[:, None, :] == jnp.arange(3)[None, :, None])
-    number = jnp.arange(256).reshape(16, 1, 16)
-    slots = jnp.max(jnp.where(picks, number, -1), axis=2).reshape(48)
     return attend_call(listed, slots, cache, absorbed, value_up, decoded)
 
 

time: 65 us -> 55.8 us (0.86)
  local copies, waits for them, and re-layouts: 4.33 us -> 0 us
  Pallas kernels: 58.4 us -> 54.9 us
  other arithmetic: 1.03 us -> 0 us
    pallas_call x1, Pallas kernels: 44.3 us -> 41.5 us  [gather_call(): pl.pallas_call(gather_kernel, out_shape=(pltpu.VMEM((4, 4, 4, 2, 18, 16,...]
    reshape x5 -> x0, local copies, waits for them, and re-layouts: 2.42 us -> none  [the longest x1 0.78 us: on_device(): step_nope.reshape(8, 2048)]
    unnamed x6 -> x0, local copies, waits for them, and re-layouts: 1.59 us -> none
    eq x1 -> x0, other arithmetic: 0.7 us -> none  [on_device(): owned = page_owner.reshape(16, 16) == dec]
    pallas_call x1, Pallas kernels: 14.2 us -> 13.5 us  [attend_call(): pl.pallas_call(attend_kernel, out_shape=(jax.ShapeDtypeStruct((512, 2048)...]
where the time goes in v2:
time: 55.8 us; the launch traced here: 55.7 us
  Pallas kernels  54.9 us (98%)
  between operations  0.8 us (1%)
    pallas_call x1, Pallas kernels, gather_call(): pl.pallas_call(gather_kernel, out_shape=(pltpu.VMEM((4, 4, 4, 2, 18, 16,...  41.5 us
    pallas_call x1, Pallas kernels, attend_call(): pl.pallas_call(attend_kernel, out_shape=(jax.ShapeDtypeStruct((512, 2048)...  13.5 us

profile of v2, /device:TPU:1, one launch (start us, length us, event | category | flops | bytes accessed | tf_op | source)
XLA Modules:
  0.0 55.7 jit_solution(9270620401083634401)
XLA Ops:
  0.6 41.5 %gather_absorb_decode.1 = (bf16[4,4,4,2,18,16,128]{6,5,4,3,2,1,0:T(8,128)(2,1)S(1)}, bf16[16,16,32,640]{3,2,1,0:T(8,128)(2,1)S(1)}, f32[16,8,512]{2,1,0:T(8,128)S(1)}, s32[4,256]{1,0:T(4,128)S(4)}, s32[8,128]{1,0:T(8,128)S(4)}) custom-call(s32[4]{0:T(128)} %prefix_in.1, bf16[64,576]{1,0:T(8,128)(2,1)} %latent_in.1, s32[8,4,256]{2,1,0:T(4,128)} %bitcast.2, ...), custom_call_target="tpu_custom_call" | custom-call | flops 4294967296 | bytes 33554432 | tf_op jit(solution)/shard_map/gather_absorb_decode/pallas_call | solution.py:472
  42.1 13.5 %attend.1 = (bf16[512,2048]{1,0:T(8,128)(2,1)}, bf16[1,48,32,576]{3,2,1,0:T(8,128)(2,1)}, bf16[4,2,2048]{2,1,0:T(2,128)(2,1)}) custom-call(s32[4,256]{1,0:T(4,128)S(4)} %get-tuple-element.8.listed, s32[8,128]{1,0:T(8,128)S(4)} %get-tuple-element.9.slots, bf16[4,4,4,2,18,16,128]{6,5,4,3,2,1,0:T(8,128)(2,1)S(1)} %get-tuple-element.10.cache, ...), custom_call_target="tpu_custom_call" | custom-call | flops 6442450944 | bytes 20971520 | tf_op jit(solution)/shard_map/attend/pallas_call | solution.py:520

commit v3 on v2

--- a/solution.py
+++ b/solution.py
@@ -195,8 +195,6 @@
 VB = 4
 SLASH = 2
 UNROLL = 4
-QUANTA = 1
-REL = (0, 1, -1, 2)
 EXP2 = 192.0 ** -0.5 * 1.4426950408889634
 NEG = float("-inf")
 
@@ -235,8 +233,8 @@
 
 def gather_kernel(
     prefix_in, latent_in, lists_in, owner_in, nope_in, rope_in, fresh_in, query_nope, query_rope, key_up,
-    cache, absorbed, decoded, listed, slots,
-    prefix, latent, owner, step_nope, step_rope, step_latent, tiles, qn, qr, ku, sn, sl, dq, acc, top, total, slot_rows,
+    cache, absorbed, step_queries, acc, top, total, listed, slots, prefix,
+    latent, owner, step_nope, step_rope, step_latent, tiles, qn, qr, ku, sn, sl, dq, slot_rows,
     send, recv, local,
 ):
     t = Gather(cache, send, recv)
@@ -294,6 +292,7 @@
             rope = sn[:, 2048 + 64 * h : 2048 + 64 * h + 64]
             dq[h, :, 512:] = jnp.concatenate([rope, rope], axis=1)
         q = dq[...].reshape(128, 640).astype(jnp.bfloat16)
+        step_queries[...] = q
         fresh = sl[...].astype(jnp.bfloat16)
         s = dot_t(q[:, :576], fresh)
         row = lax.broadcasted_iota(jnp.int32, (128, 8), 0) % 8
@@ -305,42 +304,7 @@
         total[...] = jnp.broadcast_to(jnp.sum(e, axis=1, keepdims=True), (128, 128))
         acc[...] = dot(e.astype(jnp.bfloat16), fresh[:, :512])
 
-    def decode(places):
-        n = 128 * len(places)
-        blocks, homes = [], []
-        for place in places:
-            t.take(place)
-            y, z, x = (t.spot(axis, place[axis]) for axis in ("y", "z", "x"))
-            blocks.append(cache[y, z, x].reshape(4, 9, 16, 128))
-            homes.append(lax.broadcasted_iota(jnp.int32, (128, 128), 1) + 128 * (16 * y + 4 * z + x))
-        values, rope = keys_from(jnp.concatenate(blocks, axis=0))
-        q = dq[...].reshape(128, 640).astype(jnp.bfloat16)
-        s = dot_t(q, jnp.concatenate([values, rope], axis=1))
-        row = lax.broadcasted_iota(jnp.int32, (128, n), 0) % 8 // 2
-        limit = jnp.where(row == 0, prefix[0], jnp.where(row == 1, prefix[1], jnp.where(row == 2, prefix[2], prefix[3])))
-        place = jnp.concatenate(homes, axis=1)
-        s = jnp.where(place < limit, s, NEG)
-        before = top[:, :1]
-        m = jnp.maximum(before, jnp.max(s, axis=1, keepdims=True))
-        keep = jnp.exp2((before - m) * EXP2)
-        e = jnp.exp2((s - m) * EXP2)
-        top[...] = jnp.broadcast_to(m, (128, 128))
-        total[...] = total[...] * keep + jnp.sum(e, axis=1, keepdims=True)
-        acc[...] = acc[...] * keep + dot(e.astype(jnp.bfloat16), values)
-
-    waiting = [dict(x=x, y=y, z=z) for x in REL for y in REL for z in REL]
-    waiting.sort(key=complete_at)
-    here = -1
-
-    def decode_some(most, all_of=False):
-        for _ in range(most):
-            ready = [p for p in waiting if complete_at(p) <= here]
-            if len(ready) >= 4 or (all_of and ready):
-                decode(ready[:4])
-                del waiting[: len(ready[:4])]
-
-    step = 0
-    for mark in t.steps():
+    for step, _ in enumerate(t.steps()):
         if step == 0:
             for c in loads:
                 c.wait()
@@ -352,22 +316,15 @@
             absorb(2 * step + 1)
         elif step == 8:
             decode_start()
-            own_copy.wait()
-        if mark in MARKS:
-            here = MARKS.index(mark)
-        if here >= 0:
-            decode_some(QUANTA)
-        step += 1
-    decode_some(64, True)
+    own_copy.wait()
     t.finish()
     out_slots.wait()
-    decoded[...] = (acc[...] / total[:, :1]).reshape(16, 8, 512)
 
 
 def attend_kernel(
-    listed, slots, cache, absorbed, value_up, decoded,
+    listed, slots, prefix, cache, absorbed, step_queries, acc_in, top_in, total_in, value_up,
     prefill_out, paged, decode_out,
-    vu, ctx, out, paged_hold,
+    vu, ctx, out, paged_hold, acc, top, total, step_out,
     s_in, s_out, s_paged,
 ):
     seq = lax.axis_index("seq")
@@ -435,28 +392,60 @@
         part = pl.ds(k * group, group)
         return pltpu.make_async_copy(paged_hold.at[part], paged.at[0, part], s_paged.at[k])
 
+    acc[...] = acc_in[...]
+    top[...] = top_in[...]
+    total[...] = total_in[...]
+    step_row = lax.broadcasted_iota(jnp.int32, (128, 128), 0) % 8 // 2
+    limit = jnp.where(step_row == 3, prefix[3], prefix[0])
+    for b in (1, 2):
+        limit = jnp.where(step_row == b, prefix[b], limit)
+
+    def decode_score(y):
+        values, rope = keys_from(cache[y].reshape(64, 9, 16, 128))
+        s = dot_t(step_queries[...], jnp.concatenate([values, rope], axis=1))
+        place = lax.broadcasted_iota(jnp.int32, (128, 2048), 1) + 2048 * y
+        return jnp.where(place < limit[:, :1], s, NEG)
+
+    def decode_weigh(s):
+        before = top[...]
+        m = jnp.maximum(before, jnp.max(s, axis=1, keepdims=True))
+        keep = jnp.exp2((before - m) * EXP2)
+        e = jnp.exp2((s - m[:, :1]) * EXP2)
+        top[...] = m
+        total[...] = total[...] * keep + jnp.sum(e, axis=1, keepdims=True)
+        return e.astype(jnp.bfloat16), keep[:, :1]
+
+    def decode_mix(y, e, keep):
+        values = keys_from(cache[y].reshape(64, 9, 16, 128))[0]
+        acc[...] = acc[...] * keep + dot(e, values)
+
     @pl.loop(0, 16 // UNROLL)
     def _(k):
         turns = [k * UNROLL + u for u in range(UNROLL)]
         scores = [score(n) for n in turns]
+        ds = decode_score(k)
         weights = [weigh(s) for s in scores]
+        dw = decode_weigh(ds)
         for n, w in zip(turns, weights):
             mix(n, *w)
+        decode_mix(k, *dw)
         pages_out(k)
 
     in_vu.wait()
+    decoded = (acc[...] / total[:, :1]).reshape(16, 8, 512).astype(jnp.bfloat16)
     outs = []
     for h in range(16):
         cols = slice(128 * h, 128 * h + 128)
+        got = dot(decoded[h], vu[h]).astype(jnp.bfloat16)
+        for b in range(4):
+            step_out[b, :, cols] = got[2 * b : 2 * b + 2]
         out[:, cols] = dot(ctx[h], vu[h]).astype(jnp.bfloat16)
-        got = dot(decoded[h].astype(jnp.bfloat16), vu[h]).astype(jnp.bfloat16)
-        for b in range(4):
-            decode_out[b, :, cols] = got[2 * b : 2 * b + 2]
-        if h % 4 == 3:
-            wide = slice(128 * (h - 3), 128 * h + 128)
-            copy = pltpu.make_async_copy(out.at[:, wide], prefill_out.at[:, wide], s_out.at[h // 4])
-            copy.start()
-            outs.append(copy)
+        if h % 2 == 1:
+            wide = slice(128 * (h - 1), 128 * h + 128)
+            outs.append(pltpu.make_async_copy(out.at[:, wide], prefill_out.at[:, wide], s_out.at[h // 2]))
+            outs[-1].start()
+    outs.append(pltpu.make_async_copy(step_out, decode_out, s_out.at[8]))
+    outs[-1].start()
     for copy in outs:
         copy.wait()
     for k in range(16 // UNROLL):
@@ -474,14 +463,17 @@
         out_shape=(
             pltpu.VMEM((4, 4, 4, 2, 18, 16, 128), bf16),
             pltpu.VMEM((16, 16, BLK, 640), bf16),
-            pltpu.VMEM((16, 8, 512), f32),
+            pltpu.VMEM((128, 640), bf16),
+            pltpu.VMEM((128, 512), f32),
+            pltpu.VMEM((128, 128), f32),
+            pltpu.VMEM((128, 128), f32),
             pltpu.SMEM((4, 256), i32),
             pltpu.SMEM((8, 128), i32),
+            pltpu.SMEM((4,), i32),
         ),
         in_specs=[any_] * 10,
-        out_specs=(vmem, vmem, vmem, smem, smem),
+        out_specs=(vmem,) * 6 + (smem,) * 3,
         scratch_shapes=[
-            pltpu.SMEM((4,), i32),
             pltpu.VMEM((64, 576), bf16),
             pltpu.VMEM((1, 256), i32),
             pltpu.VMEM((4, 2, 2048), bf16),
@@ -494,9 +486,6 @@
             pltpu.VMEM((8, 3072), f32),
             pltpu.VMEM((8, 576), f32),
             pltpu.VMEM((16, 8, 640), f32),
-            pltpu.VMEM((128, 512), f32),
-            pltpu.VMEM((128, 128), f32),
-            pltpu.VMEM((128, 128), f32),
             pltpu.VMEM((8, 128), i32),
             dma((COPIES,)), dma((COPIES,)), dma((12,)),
         ],
@@ -508,14 +497,12 @@
     )(*args)
 
 
-def attend_call(listed, slots, cache, absorbed, value_up, decoded):
+def attend_call(cache, absorbed, step_queries, acc, top, total, listed, slots, prefix, value_up):
     vmem, smem, any_ = (pl.BlockSpec(memory_space=m) for m in (pltpu.VMEM, pltpu.SMEM, pl.ANY))
-    bf16 = jnp.bfloat16
+    bf16, f32 = jnp.bfloat16, jnp.float32
     dma = pltpu.SemaphoreType.DMA
-    cache, absorbed, decoded = (
-        pltpu.with_memory_space_constraint(x, pltpu.VMEM) for x in (cache, absorbed, decoded)
-    )
-    listed, slots = (pltpu.with_memory_space_constraint(x, pltpu.SMEM) for x in (listed, slots))
+    large = [pltpu.with_memory_space_constraint(x, pltpu.VMEM) for x in (cache, absorbed, step_queries, acc, top, total)]
+    small = [pltpu.with_memory_space_constraint(x, pltpu.SMEM) for x in (listed, slots, prefix)]
     value_up = pltpu.with_memory_space_constraint(value_up, pltpu.HBM)
     return pl.pallas_call(
         attend_kernel,
@@ -524,30 +511,34 @@
             jax.ShapeDtypeStruct((1, 48, BLK, 576), bf16),
             jax.ShapeDtypeStruct((4, 2, 2048), bf16),
         ),
-        in_specs=[smem, smem, vmem, vmem, any_, vmem],
-        out_specs=(any_, any_, vmem),
+        in_specs=[smem] * 3 + [vmem] * 6 + [any_],
+        out_specs=(any_, any_, any_),
         scratch_shapes=[
             pltpu.VMEM((16, 512, 128), bf16),
             pltpu.VMEM((16, 512, 512), bf16),
             pltpu.VMEM((512, 2048), bf16),
             pltpu.VMEM((48, BLK, 576), bf16),
-            dma, dma((4,)), dma((4,)),
+            pltpu.VMEM((128, 512), f32),
+            pltpu.VMEM((128, 128), f32),
+            pltpu.VMEM((128, 128), f32),
+            pltpu.VMEM((4, 2, 2048), bf16),
+            dma, dma((9,)), dma((4,)),
         ],
-        compiler_params=pltpu.CompilerParams(vmem_limit_bytes=20 << 20),
-        cost_estimate=pl.CostEstimate(flops=6 << 30, bytes_accessed=20 << 20, transcendentals=2 << 20),
+        compiler_params=pltpu.CompilerParams(vmem_limit_bytes=34 << 20),
+        cost_estimate=pl.CostEstimate(flops=8 << 30, bytes_accessed=20 << 20, transcendentals=3 << 20),
         name="attend",
-    )(listed, slots, cache, absorbed, value_up, decoded)
+    )(*small, *large, value_up)
 
 
 def on_device(
     query_nope, query_rope, latent_cache, key_up, value_up, vertical_lists, page_owner,
     step_nope, step_rope, step_latent, prefix_lengths,
 ):
-    cache, absorbed, decoded, listed, slots = gather_call(
+    kept = gather_call(
         prefix_lengths, latent_cache, vertical_lists.transpose(0, 2, 1), page_owner.reshape(1, 256),
         step_nope, step_rope, step_latent, query_nope, query_rope, key_up,
     )
-    return attend_call(listed, slots, cache, absorbed, value_up, decoded)
+    return attend_call(*kept, value_up)
 
 
 def solution(mesh):

time: 55.8 us -> 52.8 us (0.946)
  Pallas kernels: 54.9 us -> 52.1 us
    pallas_call x1, Pallas kernels: 41.5 us -> 34.9 us  [gather_call(): pl.pallas_call(gather_kernel, out_shape=(pltpu.VMEM((4, 4, 4, 2, 18, 16,...]
    pallas_call x1, Pallas kernels: 13.5 us -> 17.1 us  [attend_call(): pl.pallas_call(attend_kernel, out_shape=(jax.ShapeDtypeStruct((512, 2048)...]
where the time goes in v3:
time: 52.8 us; the launch traced here: 52.7 us
  Pallas kernels  52.1 us (99%)
  between operations  0.64 us (1%)
    pallas_call x1, Pallas kernels, gather_call(): pl.pallas_call(gather_kernel, out_shape=(pltpu.VMEM((4, 4, 4, 2, 18, 16,...  34.9 us
    pallas_call x1, Pallas kernels, attend_call(): pl.pallas_call(attend_kernel, out_shape=(jax.ShapeDtypeStruct((512, 2048)...  17.1 us

profile of v3, /device:TPU:1, one launch (start us, length us, event | category | flops | bytes accessed | tf_op | source)
XLA Modules:
  0.0 52.7 jit_solution(296353239588144848)
XLA Ops:
  0.6 34.9 %gather_absorb_decode.1 = (bf16[4,4,4,2,18,16,128]{6,5,4,3,2,1,0:T(8,128)(2,1)S(1)}, bf16[16,16,32,640]{3,2,1,0:T(8,128)(2,1)S(1)}, bf16[128,640]{1,0:T(8,128)(2...) custom-call(s32[4]{0:T(128)} %prefix_in.1, ...), custom_call_target="tpu_custom_call" | custom-call | flops 4294967296 | bytes 33554432 | tf_op jit(solution)/shard_map/gather_absorb_decode/pallas_call | solution.py:461
  35.6 17.1 %attend.1 = (bf16[512,2048]{1,0:T(8,128)(2,1)}, bf16[1,48,32,576]{3,2,1,0:T(8,128)(2,1)}, bf16[4,2,2048]{2,1,0:T(2,128)(2,1)}) custom-call(s32[4,256]{1,0:T(4,128)S(4)} %get-tuple-element.12.listed, s32[8,128]{1,0:T(8,128)S(4)} %get-tuple-element.13.slots, s32[4]{0:T(128)S(4)} %get-tuple-element.14.prefix, ...), custom_call_target="tpu_custom_call" | custom-call | flops 8589934592 | bytes 20971520 | tf_op jit(solution)/shard_map/attend/pallas_call | solution.py:507

commit v4 on v3

--- a/solution.py
+++ b/solution.py
@@ -197,6 +197,9 @@
 UNROLL = 4
 EXP2 = 192.0 ** -0.5 * 1.4426950408889634
 NEG = float("-inf")
+LEAST = -3.0e38
+REL = (0, 1, -1, 2)
+PLAN = {(2, 1): 24, (-1, 2): 24}
 
 
 def dot(a, b):
@@ -233,8 +236,8 @@
 
 def gather_kernel(
     prefix_in, latent_in, lists_in, owner_in, nope_in, rope_in, fresh_in, query_nope, query_rope, key_up,
-    cache, absorbed, step_queries, acc, top, total, listed, slots, prefix,
-    latent, owner, step_nope, step_rope, step_latent, tiles, qn, qr, ku, sn, sl, dq, slot_rows,
+    cache, absorbed, mine, theirs, listed, slots, prefix,
+    latent, owner, step_nope, step_rope, step_latent, tiles, qn, qr, ku, sn, sl, dq, queries, gone, acc, top, total, slot_rows,
     send, recv, local,
 ):
     t = Gather(cache, send, recv)
@@ -291,20 +294,66 @@
             dq[h, :, :512] = dot(sn[:, 128 * h : 128 * h + 128].astype(jnp.bfloat16), ku[h])
             rope = sn[:, 2048 + 64 * h : 2048 + 64 * h + 64]
             dq[h, :, 512:] = jnp.concatenate([rope, rope], axis=1)
-        q = dq[...].reshape(128, 640).astype(jnp.bfloat16)
-        step_queries[...] = q
+        queries[0] = dq[...].reshape(128, 640).astype(jnp.bfloat16)
+        ask.start()
+
+    def decode_fresh():
         fresh = sl[...].astype(jnp.bfloat16)
-        s = dot_t(q[:, :576], fresh)
+        s = dot_t(queries[0, :, :576], fresh)
         row = lax.broadcasted_iota(jnp.int32, (128, 8), 0) % 8
         key = lax.broadcasted_iota(jnp.int32, (128, 8), 1)
         s = jnp.where((row // 2 == key // 2) & (key <= row), s, NEG)
         m = jnp.max(s, axis=1, keepdims=True)
         e = jnp.exp2((s - m) * EXP2)
-        top[...] = jnp.broadcast_to(m, (128, 128))
-        total[...] = jnp.broadcast_to(jnp.sum(e, axis=1, keepdims=True), (128, 128))
-        acc[...] = dot(e.astype(jnp.bfloat16), fresh[:, :512])
-
-    for step, _ in enumerate(t.steps()):
+        top[:128] = jnp.broadcast_to(m, (128, 128))
+        total[:128] = jnp.broadcast_to(jnp.sum(e, axis=1, keepdims=True), (128, 128))
+        acc[:128] = dot(e.astype(jnp.bfloat16), fresh[:, :512])
+        top[128:] = jnp.full((128, 128), LEAST)
+        total[128:] = jnp.zeros((128, 128), jnp.float32)
+        acc[128:] = jnp.zeros((128, 512), jnp.float32)
+
+    def decode(places):
+        blocks, homes = [], []
+        half = lax.broadcasted_iota(jnp.int32, (1, 128), 1)
+        for i, place in enumerate(places):
+            y, z, x = (t.spot(axis, place[axis]) for axis in ("y", "z", "x"))
+            blocks.append(cache[y, z, x, t.core].reshape(2, 9, 16, 128))
+            homes.append(512 * (4 * y + z) + 128 * x + 64 * t.core)
+        place = jnp.concatenate(
+            [jnp.where(half < 64, homes[i] + half, homes[i + 1] + half - 64) for i in range(0, len(homes), 2)], axis=1
+        )
+        values, rope = keys_from(jnp.concatenate(blocks, axis=0))
+        q = queries[...].reshape(256, 640)
+        s = dot_t(q, jnp.concatenate([values, rope], axis=1))
+        row = lax.broadcasted_iota(jnp.int32, (256, 1), 0) % 8 // 2
+        limit = jnp.where(row == 3, prefix[3], prefix[0])
+        for b in (1, 2):
+            limit = jnp.where(row == b, prefix[b], limit)
+        s = jnp.where(place < limit, s, NEG)
+        before = top[...]
+        m = jnp.maximum(before, jnp.max(s, axis=1, keepdims=True))
+        keep = jnp.exp2((before - m) * EXP2)
+        e = jnp.exp2((s - m[:, :1]) * EXP2)
+        top[...] = m
+        total[...] = total[...] * keep + jnp.sum(e, axis=1, keepdims=True)
+        acc[...] = acc[...] * keep[:, :1] + dot(e.astype(jnp.bfloat16), values)
+
+    def mate_copy(k, src, dst):
+        return pltpu.make_async_remote_copy(
+            src_ref=src, dst_ref=dst, send_sem=send.at[COPIES + k], recv_sem=recv.at[COPIES + k],
+            device_id=t.device(mate=True), device_id_type=MESH)
+
+    ask = mate_copy(0, queries.at[0], queries.at[1])
+    answer = mate_copy(1, gone, theirs)
+
+    waiting = [dict(x=x, y=y, z=z) for x in REL for y in REL for z in REL]
+    waiting.sort(key=complete_at)
+
+    def decode_next(size):
+        decode(waiting[:size])
+        del waiting[:size]
+
+    for step, mark in enumerate(t.steps()):
         if step == 0:
             for c in loads:
                 c.wait()
@@ -316,15 +365,32 @@
             absorb(2 * step + 1)
         elif step == 8:
             decode_start()
-    own_copy.wait()
+        elif step == 9:
+            decode_fresh()
+            own_copy.wait()
+            ask.wait()
+        size = PLAN.get(mark, 0)
+        if size:
+            assert all(MARKS.index(mark) >= complete_at(p) for p in waiting[:size])
+            decode_next(size)
+    while waiting:
+        decode_next(min(len(waiting), 16))
+    gone[:, :512] = acc[128:]
+    gone[:, 512:640] = top[128:]
+    gone[:, 640:] = total[128:]
+    answer.start()
+    mine[:, :512] = acc[:128]
+    mine[:, 512:640] = top[:128]
+    mine[:, 640:] = total[:128]
     t.finish()
     out_slots.wait()
+    answer.wait()
 
 
 def attend_kernel(
-    listed, slots, prefix, cache, absorbed, step_queries, acc_in, top_in, total_in, value_up,
+    listed, slots, cache, absorbed, mine, theirs, value_up,
     prefill_out, paged, decode_out,
-    vu, ctx, out, paged_hold, acc, top, total, step_out,
+    vu, ctx, out, paged_hold, step_out,
     s_in, s_out, s_paged,
 ):
     seq = lax.axis_index("seq")
@@ -392,47 +458,21 @@
         part = pl.ds(k * group, group)
         return pltpu.make_async_copy(paged_hold.at[part], paged.at[0, part], s_paged.at[k])
 
-    acc[...] = acc_in[...]
-    top[...] = top_in[...]
-    total[...] = total_in[...]
-    step_row = lax.broadcasted_iota(jnp.int32, (128, 128), 0) % 8 // 2
-    limit = jnp.where(step_row == 3, prefix[3], prefix[0])
-    for b in (1, 2):
-        limit = jnp.where(step_row == b, prefix[b], limit)
-
-    def decode_score(y):
-        values, rope = keys_from(cache[y].reshape(64, 9, 16, 128))
-        s = dot_t(step_queries[...], jnp.concatenate([values, rope], axis=1))
-        place = lax.broadcasted_iota(jnp.int32, (128, 2048), 1) + 2048 * y
-        return jnp.where(place < limit[:, :1], s, NEG)
-
-    def decode_weigh(s):
-        before = top[...]
-        m = jnp.maximum(before, jnp.max(s, axis=1, keepdims=True))
-        keep = jnp.exp2((before - m) * EXP2)
-        e = jnp.exp2((s - m[:, :1]) * EXP2)
-        top[...] = m
-        total[...] = total[...] * keep + jnp.sum(e, axis=1, keepdims=True)
-        return e.astype(jnp.bfloat16), keep[:, :1]
-
-    def decode_mix(y, e, keep):
-        values = keys_from(cache[y].reshape(64, 9, 16, 128))[0]
-        acc[...] = acc[...] * keep + dot(e, values)
-
     @pl.loop(0, 16 // UNROLL)
     def _(k):
         turns = [k * UNROLL + u for u in range(UNROLL)]
         scores = [score(n) for n in turns]
-        ds = decode_score(k)
         weights = [weigh(s) for s in scores]
-        dw = decode_weigh(ds)
         for n, w in zip(turns, weights):
             mix(n, *w)
-        decode_mix(k, *dw)
         pages_out(k)
 
     in_vu.wait()
-    decoded = (acc[...] / total[:, :1]).reshape(16, 8, 512).astype(jnp.bfloat16)
+    m = jnp.maximum(mine[:, 512:640], theirs[:, 512:640])
+    here, there = jnp.exp2((mine[:, 512:640] - m) * EXP2), jnp.exp2((theirs[:, 512:640] - m) * EXP2)
+    both = mine[:, 640:] * here + theirs[:, 640:] * there
+    decoded = (mine[:, :512] * here[:, :1] + theirs[:, :512] * there[:, :1]) / both[:, :1]
+    decoded = decoded.reshape(16, 8, 512).astype(jnp.bfloat16)
     outs = []
     for h in range(16):
         cols = slice(128 * h, 128 * h + 128)
@@ -463,16 +503,14 @@
         out_shape=(
             pltpu.VMEM((4, 4, 4, 2, 18, 16, 128), bf16),
             pltpu.VMEM((16, 16, BLK, 640), bf16),
-            pltpu.VMEM((128, 640), bf16),
-            pltpu.VMEM((128, 512), f32),
-            pltpu.VMEM((128, 128), f32),
-            pltpu.VMEM((128, 128), f32),
+            pltpu.VMEM((128, 768), f32),
+            pltpu.VMEM((128, 768), f32),
             pltpu.SMEM((4, 256), i32),
             pltpu.SMEM((8, 128), i32),
             pltpu.SMEM((4,), i32),
         ),
         in_specs=[any_] * 10,
-        out_specs=(vmem,) * 6 + (smem,) * 3,
+        out_specs=(vmem,) * 4 + (smem,) * 3,
         scratch_shapes=[
             pltpu.VMEM((64, 576), bf16),
             pltpu.VMEM((1, 256), i32),
@@ -486,23 +524,28 @@
             pltpu.VMEM((8, 3072), f32),
             pltpu.VMEM((8, 576), f32),
             pltpu.VMEM((16, 8, 640), f32),
+            pltpu.VMEM((2, 128, 640), bf16),
+            pltpu.VMEM((128, 768), f32),
+            pltpu.VMEM((256, 512), f32),
+            pltpu.VMEM((256, 128), f32),
+            pltpu.VMEM((256, 128), f32),
             pltpu.VMEM((8, 128), i32),
-            dma((COPIES,)), dma((COPIES,)), dma((12,)),
+            dma((COPIES + 2,)), dma((COPIES + 2,)), dma((12,)),
         ],
         compiler_params=pltpu.CompilerParams(
-            collective_id=0, has_side_effects=True, vmem_limit_bytes=16 << 20
+            collective_id=0, has_side_effects=True, vmem_limit_bytes=24 << 20
         ),
         cost_estimate=pl.CostEstimate(flops=4 << 30, bytes_accessed=32 << 20, transcendentals=1 << 20),
         name="gather_absorb_decode",
     )(*args)
 
 
-def attend_call(cache, absorbed, step_queries, acc, top, total, listed, slots, prefix, value_up):
+def attend_call(cache, absorbed, mine, theirs, listed, slots, prefix, value_up):
     vmem, smem, any_ = (pl.BlockSpec(memory_space=m) for m in (pltpu.VMEM, pltpu.SMEM, pl.ANY))
     bf16, f32 = jnp.bfloat16, jnp.float32
     dma = pltpu.SemaphoreType.DMA
-    large = [pltpu.with_memory_space_constraint(x, pltpu.VMEM) for x in (cache, absorbed, step_queries, acc, top, total)]
-    small = [pltpu.with_memory_space_constraint(x, pltpu.SMEM) for x in (listed, slots, prefix)]
+    large = [pltpu.with_memory_space_constraint(x, pltpu.VMEM) for x in (cache, absorbed, mine, theirs)]
+    small = [pltpu.with_memory_space_constraint(x, pltpu.SMEM) for x in (listed, slots)]
     value_up = pltpu.with_memory_space_constraint(value_up, pltpu.HBM)
     return pl.pallas_call(
         attend_kernel,
@@ -511,20 +554,17 @@
             jax.ShapeDtypeStruct((1, 48, BLK, 576), bf16),
             jax.ShapeDtypeStruct((4, 2, 2048), bf16),
         ),
-        in_specs=[smem] * 3 + [vmem] * 6 + [any_],
+        in_specs=[smem] * 2 + [vmem] * 4 + [any_],
         out_specs=(any_, any_, any_),
         scratch_shapes=[
             pltpu.VMEM((16, 512, 128), bf16),
             pltpu.VMEM((16, 512, 512), bf16),
             pltpu.VMEM((512, 2048), bf16),
             pltpu.VMEM((48, BLK, 576), bf16),
-            pltpu.VMEM((128, 512), f32),
-            pltpu.VMEM((128, 128), f32),
-            pltpu.VMEM((128, 128), f32),
             pltpu.VMEM((4, 2, 2048), bf16),
             dma, dma((9,)), dma((4,)),
         ],
-        compiler_params=pltpu.CompilerParams(vmem_limit_bytes=34 << 20),
+        compiler_params=pltpu.CompilerParams(vmem_limit_bytes=24 << 20),
         cost_estimate=pl.CostEstimate(flops=8 << 30, bytes_accessed=20 << 20, transcendentals=3 << 20),
         name="attend",
     )(*small, *large, value_up)

time: 52.8 us -> 49.8 us (0.943)
  Pallas kernels: 52.1 us -> 49.1 us
    pallas_call x1, Pallas kernels: 17.1 us -> 12.7 us  [attend_call(): pl.pallas_call(attend_kernel, out_shape=(jax.ShapeDtypeStruct((512, 2048)...]
    pallas_call x1, Pallas kernels: 34.9 us -> 36.3 us  [gather_call(): pl.pallas_call(gather_kernel, out_shape=(pltpu.VMEM((4, 4, 4, 2, 18, 16,...]
where the time goes in v4:
time: 49.8 us; the launch traced here: 49.7 us
  Pallas kernels  49.1 us (99%)
  between operations  0.64 us (1%)
    pallas_call x1, Pallas kernels, gather_call(): pl.pallas_call(gather_kernel, out_shape=(pltpu.VMEM((4, 4, 4, 2, 18, 16,...  36.3 us
    pallas_call x1, Pallas kernels, attend_call(): pl.pallas_call(attend_kernel, out_shape=(jax.ShapeDtypeStruct((512, 2048)...  12.7 us

profile of v4, /device:TPU:1, one launch (start us, length us, event | category | flops | bytes accessed | tf_op | source)
XLA Modules:
  0.0 49.7 jit_solution(1008254743132848579)
XLA Ops:
  0.6 36.3 %gather_absorb_decode.1 = (bf16[4,4,4,2,18,16,128]{6,5,4,3,2,1,0:T(8,128)(2,1)S(1)}, bf16[16,16,32,640]{3,2,1,0:T(8,128)(2,1)S(1)}, f32[128,768]{1,0:T(8,128)S(1...) custom-call(s32[4]{0:T(128)} %prefix_in.1, ...), custom_call_target="tpu_custom_call" | custom-call | flops 4294967296 | bytes 33554432 | tf_op jit(solution)/shard_map/gather_absorb_decode/pallas_call | solution.py:501
  37.0 12.7 %attend.1 = (bf16[512,2048]{1,0:T(8,128)(2,1)}, bf16[1,48,32,576]{3,2,1,0:T(8,128)(2,1)}, bf16[4,2,2048]{2,1,0:T(2,128)(2,1)}) custom-call(s32[4,256]{1,0:T(4,128)S(4)} %get-tuple-element.9.listed, s32[8,128]{1,0:T(8,128)S(4)} %get-tuple-element.10.slots, bf16[4,4,4,2,18,16,128]{6,5,4,3,2,1,0:T(8,128)(2,1)S(1)} %get-tuple-element.11.cache, ...), custom_call_target="tpu_custom_call" | custom-call | flops 8589934592 | bytes 20971520 | tf_op jit(solution)/shard_map/attend/pallas_call | solution.py:550
